TPU v7x, 256 devices: a whole 4x4x8 slice. The times are simulated.
256 devices in a mesh: depth: 4 (over z_lo, core), scan: 64 (over z_hi, x, y).
Axes of the slice: x: 4, y: 4, z: 8 (z_hi: 4, z_lo: 2; z = z_hi * 2 + z_lo), core: 2. Of those that a mesh axis runs over, the one named last changes fastest.
Arguments:
- transmission: float32 [4, 2, 4096, 3072], P('depth', None, 'scan'), may hold values from -5 to 5
- probe: float32 [2, 256, 256], replicated, may hold values from -6 to 6
- exit_adjoint: float32 [2, 128, 2, 256, 256], P(None, 'scan'), may hold values from -6 to 6
- scan_row: int32 [2, 128], P(None, 'scan'), may hold values from 0 to 4095, as said below
- scan_col: int32 [2, 128], P(None, 'scan'), may hold values from 0 to 2816
Outputs:
- object_grad: float32 [4, 2, 4096, 3072], P('depth', None, 'scan')
- probe_grad: float32 [2, 256, 256], P(None, 'depth')
Inputs may be any that keep to these rules, and one draw needn't show every extreme that they name: `scan_row`: entries 2 * j to 2 * (j + 1) - 1 of every batch lie in rows 64 * j to 64 * (j + 1) - 1: they are the positions of scan region j.
All inputs are finite; a program needn't handle non-finite values.
Results may differ from a plain program's by a relative error of at most 0.0075.
Values may be sent and summed in bfloat16 or wider, within the bound.
A program may use at most 128 MiB of HBM per device.

v0:
```python
import math

import jax
import jax.numpy as jnp
from jax import lax
from jax.sharding import PartitionSpec as P

fresnel = 0.25


def from_behind(value, axis, by):
    length = lax.axis_size(axis)
    return lax.ppermute(value, axis, [(i, (i + by) % length) for i in range(length)])


def shifted(block, axis, distance):
    devices = range(lax.axis_size(axis))
    route = [(i - distance, i) for i in devices if i - distance in devices]
    return lax.ppermute(block, axis, route)


def tables(extent):
    highest = lax.Precision.HIGHEST
    indices = jnp.arange(extent)
    frequency = jnp.where(indices < extent // 2, indices, indices - extent).astype(jnp.float32)
    phases = -math.pi * fresnel / extent * frequency * frequency
    factor_real = jnp.cos(phases)
    factor_imag = jnp.sin(phases)
    turns = indices[:, None] * indices[None, :] % extent
    angles = 2.0 * math.pi / extent * turns.astype(jnp.float32)
    cos_table = jnp.cos(angles)
    sin_table = jnp.sin(angles)
    mixed_real = cos_table * factor_real[None, :] - sin_table * factor_imag[None, :]
    mixed_imag = cos_table * factor_imag[None, :] + sin_table * factor_real[None, :]
    prop_real = (
        jnp.dot(mixed_real, cos_table, precision=highest)
        + jnp.dot(mixed_imag, sin_table, precision=highest)
    ) / extent
    prop_imag = (
        jnp.dot(mixed_imag, cos_table, precision=highest)
        - jnp.dot(mixed_real, sin_table, precision=highest)
    ) / extent
    return (prop_real, prop_imag)


def apply_left(matrix, values):
    return jnp.einsum(
        "ma,kab->kmb",
        matrix,
        values,
        precision=lax.Precision.HIGHEST,
        preferred_element_type=jnp.float32,
    )


def apply_right(values, matrix):
    return jnp.einsum(
        "kab,nb->kan",
        values,
        matrix,
        precision=lax.Precision.HIGHEST,
        preferred_element_type=jnp.float32,
    )


def propagate(fields, prop_real, prop_imag):
    in_real = fields[:, 0]
    in_imag = fields[:, 1]
    mid_real = apply_left(prop_real, in_real) - apply_left(prop_imag, in_imag)
    mid_imag = apply_left(prop_real, in_imag) + apply_left(prop_imag, in_real)
    out_real = apply_right(mid_real, prop_real) - apply_right(mid_imag, prop_imag)
    out_imag = apply_right(mid_real, prop_imag) + apply_right(mid_imag, prop_real)
    return jnp.stack([out_real, out_imag], axis=1)


def multiply(first, second):
    real_part = first[:, 0] * second[:, 0] - first[:, 1] * second[:, 1]
    imag_part = first[:, 0] * second[:, 1] + first[:, 1] * second[:, 0]
    return jnp.stack([real_part, imag_part], axis=1)


def conj_multiply(first, second):
    real_part = first[:, 0] * second[:, 0] + first[:, 1] * second[:, 1]
    imag_part = first[:, 0] * second[:, 1] - first[:, 1] * second[:, 0]
    return jnp.stack([real_part, imag_part], axis=1)


def extract(extended, layer, row_block, col_block, patch_side):

    def cut_one(row_start, col_start):
        return lax.dynamic_slice(
            extended[layer], (0, row_start, col_start), (2, patch_side, patch_side)
        )

    return jax.vmap(cut_one)(row_block, col_block)


def deposit(gradient, layer, row_block, col_block, pieces):
    patch_side = pieces.shape[2]

    def place(position, buffer_now):
        anchor = (layer, 0, row_block[position], col_block[position])
        before = lax.dynamic_slice(buffer_now, anchor, (1, 2, patch_side, patch_side))
        return lax.dynamic_update_slice(buffer_now, before + pieces[position][None], anchor)

    return lax.fori_loop(0, pieces.shape[0], place, gradient)


def local(transmission, probe, exit_adjoint, scan_row, scan_col):
    layers = transmission.shape[0]
    strip_rows = transmission.shape[2]
    columns = transmission.shape[3]
    patch_side = probe.shape[1]
    rim_count = patch_side // strip_rows
    section_count = lax.axis_size("depth")
    section_index = lax.axis_index("depth")
    region_index = lax.axis_index("scan")
    following = []
    for region_step in range(1, rim_count + 1):
        following.append(from_behind(transmission, "scan", -region_step))
    extended = jnp.concatenate([transmission] + following, axis=2)
    prop_real, prop_imag = tables(patch_side)
    local_rows = scan_row - region_index * strip_rows
    batches, per_batch = scan_row.shape
    step_count = batches + section_count - 1
    probe_block = jnp.broadcast_to(probe, (per_batch, 2, patch_side, patch_side))

    def forward(step_index, state_pair):
        incoming, saved_waves = state_pair
        micro_index = step_index - section_index
        is_active = (micro_index >= 0) & (micro_index < batches)
        slot_index = jnp.clip(micro_index, 0, batches - 1)
        wave_now = jnp.where(section_index == 0, probe_block, incoming.astype(jnp.float32))
        row_block = local_rows[slot_index]
        col_block = scan_col[slot_index]
        incident = [wave_now]
        local_patch = extract(extended, 0, row_block, col_block, patch_side)
        wave_now = propagate(multiply(local_patch, wave_now), prop_real, prop_imag)
        new_entry = jnp.where(is_active, jnp.stack(incident), saved_waves[slot_index])
        saved_waves = lax.dynamic_update_index_in_dim(saved_waves, new_entry, slot_index, 0)
        incoming = shifted(wave_now.astype(jnp.bfloat16), "depth", 1)
        return (incoming, saved_waves)

    start_incoming = jnp.zeros((per_batch, 2, patch_side, patch_side), jnp.bfloat16)
    start_saved = jnp.zeros((batches, layers, per_batch, 2, patch_side, patch_side), jnp.float32)
    unused_wave, saved_waves = lax.fori_loop(0, step_count, forward, (start_incoming, start_saved))

    def backward(step_index, state_triple):
        incoming, gradient, probe_total = state_triple
        micro_index = step_index - (section_count - 1 - section_index)
        is_active = (micro_index >= 0) & (micro_index < batches)
        slot_index = jnp.clip(micro_index, 0, batches - 1)
        active_weight = is_active.astype(jnp.float32)
        adjoint_now = jnp.where(
            section_index == section_count - 1,
            exit_adjoint[slot_index],
            incoming.astype(jnp.float32),
        )
        row_block = local_rows[slot_index]
        col_block = scan_col[slot_index]
        for layer in reversed(range(layers)):
            spread_back = propagate(adjoint_now, prop_real, -prop_imag)
            local_patch = extract(extended, layer, row_block, col_block, patch_side)
            update_piece = (
                conj_multiply(saved_waves[slot_index, layer], spread_back) * active_weight
            )
            gradient = deposit(gradient, layer, row_block, col_block, update_piece)
            adjoint_now = conj_multiply(local_patch, spread_back)
        probe_total = probe_total + jnp.where(
            is_active & (section_index == 0), jnp.sum(adjoint_now, axis=0), 0.0
        )
        incoming = shifted(adjoint_now.astype(jnp.bfloat16), "depth", -1)
        return (incoming, gradient, probe_total)

    start_grad = jnp.zeros((layers, 2, strip_rows + patch_side, columns), jnp.float32)
    start_probe = jnp.zeros((2, patch_side, patch_side), jnp.float32)
    unused_adjoint, gradient, probe_total = lax.fori_loop(
        0, step_count, backward, (start_incoming, start_grad, start_probe)
    )
    object_grad = gradient[:, :, :strip_rows, :]
    for region_step in range(1, rim_count + 1):
        lower_piece = gradient[:, :, region_step * strip_rows : (region_step + 1) * strip_rows, :]
        object_grad = object_grad + from_behind(
            lower_piece.astype(jnp.bfloat16), "scan", region_step
        ).astype(lower_piece.dtype)
    partial_total = lax.psum(probe_total, "scan")
    probe_grad = lax.psum_scatter(
        partial_total.astype(jnp.bfloat16), "depth", scatter_dimension=1, tiled=True
    ).astype(jnp.float32)
    return (object_grad, probe_grad)


def solution(mesh):
    placed = (
        P("depth", None, "scan", None),
        P(),
        P(None, "scan", None, None, None),
        P(None, "scan"),
        P(None, "scan"),
    )
    return jax.shard_map(
        local,
        mesh=mesh,
        in_specs=placed,
        out_specs=(P("depth", None, "scan", None), P(None, "depth", None)),
        check_vma=False,
    )
```

profile of v0, /device:TPU:4, one launch (start us, length us, event | category | flops | bytes accessed | tf_op | source)
XLA Modules:
  0.0 1247.8 jit_solution(15172315834707370760)
XLA Ops:
  8.8 2.9 collective-permute-start.3
  13.1 8.5 collective-permute-start.5
  27.7 84.8 %collective-permute-done.2 = f32[1,2,64,3072]{3,2,1,0:T(8,128)} collective-permute-done((f32[1,2,64,3072]{3,2,1,0:T(8,128)}, f32[1,2,64,3072]{3,2,1,0:T(8,128)}, u32[]{:S(2)}, u32[]{:S(2)}) %collective-permute-start.2) | collective-permute-done | bytes 1572896 | tf_op jit(solution)/shard_map/ppermute | solution.py:13
  117.0 29.9 %collective-permute-done.5 = f32[1,2,64,3072]{3,2,1,0:T(8,128)} collective-permute-done((f32[1,2,64,3072]{3,2,1,0:T(8,128)}, f32[1,2,64,3072]{3,2,1,0:T(8,128)}, u32[]{:S(2)}, u32[]{:S(2)}) %collective-permute-start.5) | collective-permute-done | bytes 1572896 | tf_op jit(solution)/shard_map/ppermute | solution.py:13
  152.1 138.2 %while.72 = (s32[]{:T(128)}, bf16[2,2,256,256]{3,2,0,1:T(8,128)(2,1)S(1)}, f32[2,1,2,2,256,256]{5,4,2,3,1,0:T(8,128)}, f32[1,2,320,3072]{3,2,1,0:T(8,128)}, s32[...) while((s32[]{:T(128)}, ...), condition=%wide.region_1.2_spmd.clone, body=%wide.region_0.1_spmd.clone.sunk | while | flops 3223846912 | bytes 25691188 | solution.py:146
  153.6 6.7 while.76
  154.3 2.7 bitcast_dynamic-update-slice_fusion.8
  157.6 2.7 bitcast_dynamic-update-slice_fusion.8
  175.0 6.7 while.76
  175.7 2.7 bitcast_dynamic-update-slice_fusion.8
  192.2 9.2 collective-permute-start.1
  204.3 6.7 while.76
  205.0 2.7 bitcast_dynamic-update-slice_fusion.8
  208.3 2.7 bitcast_dynamic-update-slice_fusion.8
  221.5 9.0 collective-permute-start.1
  233.5 6.7 while.76
  234.1 2.7 bitcast_dynamic-update-slice_fusion.8
  250.7 9.0 collective-permute-start.1
  262.6 6.7 while.76
  263.3 2.7 bitcast_dynamic-update-slice_fusion.8
  279.8 9.0 collective-permute-start.1
  291.1 4.1 broadcast_in_dim.53
  295.2 277.1 %while.75 = (s32[]{:T(128)}, bf16[2,2,256,256]{3,2,0,1:T(8,128)(2,1)}, f32[1,2,320,3072]{3,2,1,0:T(8,128)}, f32[2,256,256]{2,1,0:T(8,128)}, f32[1,2,320,3072]{3,...) while((s32[]{:T(128)}, ...), condition=%wide.region_6.7_spmd.clone, body=%wide.region_2.6_spmd.clone.sunk | while | flops 3225550848 | bytes 49809460 | solution.py:177
  307.8 8.4 while.77
  308.5 3.5 bitcast_dynamic-update-slice_fusion.7
  312.7 3.5 bitcast_dynamic-update-slice_fusion.7
  317.6 3.2 add_bitcast_fusion.2
  324.2 25.5 %while.78 = (s32[]{:T(128)}, f32[1,2,320,3072]{3,2,1,0:T(8,128)}, s32[2]{0:T(128)S(1)}, s32[2]{0:T(128)S(1)}, f32[2,2,256,256]{3,2,0,1:T(8,128)S(1)}, /*index=5*/s32[]{:T(128)}, s32[]{:T(128)}, s32[]{:T(128)}, s32[]{:T(128)}) while((s32[]{:T(128)}, f32[1,2,320,3072]{3,2,1,0:T(8,128)}, s32[2]{0:T(128)S(1)}, s32[2]{0:T(128)S(1)}, ...), condition=%wide.region_4.4_spmd, body=%wide.region_3.3_spmd.sunk | while | flops 131080 | bytes 2621649 | solution.py:106
  330.7 6.4 dynamic_update_slice.21
  343.5 6.2 dynamic_update_slice.21
  363.3 8.4 while.77
  364.0 3.5 bitcast_dynamic-update-slice_fusion.7
  368.1 3.5 bitcast_dynamic-update-slice_fusion.7
  373.0 3.2 add_bitcast_fusion.2
  379.6 25.5 %while.78 = (s32[]{:T(128)}, f32[1,2,320,3072]{3,2,1,0:T(8,128)}, s32[2]{0:T(128)S(1)}, s32[2]{0:T(128)S(1)}, f32[2,2,256,256]{3,2,0,1:T(8,128)S(1)}, /*index=5*/s32[]{:T(128)}, s32[]{:T(128)}, s32[]{:T(128)}, s32[]{:T(128)}) while((s32[]{:T(128)}, f32[1,2,320,3072]{3,2,1,0:T(8,128)}, s32[2]{0:T(128)S(1)}, s32[2]{0:T(128)S(1)}, ...), condition=%wide.region_4.4_spmd, body=%wide.region_3.3_spmd.sunk | while | flops 131080 | bytes 2621649 | solution.py:106
  386.1 6.4 dynamic_update_slice.21
  398.9 6.2 dynamic_update_slice.21
  418.7 8.4 while.77
  419.4 3.5 bitcast_dynamic-update-slice_fusion.7
  423.6 3.5 bitcast_dynamic-update-slice_fusion.7
  428.4 3.2 add_bitcast_fusion.2
  435.1 25.5 %while.78 = (s32[]{:T(128)}, f32[1,2,320,3072]{3,2,1,0:T(8,128)}, s32[2]{0:T(128)S(1)}, s32[2]{0:T(128)S(1)}, f32[2,2,256,256]{3,2,0,1:T(8,128)S(1)}, /*index=5*/s32[]{:T(128)}, s32[]{:T(128)}, s32[]{:T(128)}, s32[]{:T(128)}) while((s32[]{:T(128)}, f32[1,2,320,3072]{3,2,1,0:T(8,128)}, s32[2]{0:T(128)S(1)}, s32[2]{0:T(128)S(1)}, ...), condition=%wide.region_4.4_spmd, body=%wide.region_3.3_spmd.sunk | while | flops 131080 | bytes 2621649 | solution.py:106
  441.6 6.4 dynamic_update_slice.21
  454.4 6.2 dynamic_update_slice.21
  474.2 8.4 while.77
  474.9 3.5 bitcast_dynamic-update-slice_fusion.7
  479.1 3.5 bitcast_dynamic-update-slice_fusion.7
  483.9 3.2 add_bitcast_fusion.2
  490.6 25.5 %while.78 = (s32[]{:T(128)}, f32[1,2,320,3072]{3,2,1,0:T(8,128)}, s32[2]{0:T(128)S(1)}, s32[2]{0:T(128)S(1)}, f32[2,2,256,256]{3,2,0,1:T(8,128)S(1)}, /*index=5*/s32[]{:T(128)}, s32[]{:T(128)}, s32[]{:T(128)}, s32[]{:T(128)}) while((s32[]{:T(128)}, f32[1,2,320,3072]{3,2,1,0:T(8,128)}, s32[2]{0:T(128)S(1)}, s32[2]{0:T(128)S(1)}, ...), condition=%wide.region_4.4_spmd, body=%wide.region_3.3_spmd.sunk | while | flops 131080 | bytes 2621649 | solution.py:106
  497.0 6.4 dynamic_update_slice.21
  509.8 6.2 dynamic_update_slice.21
  529.6 8.4 while.77
  530.3 3.5 bitcast_dynamic-update-slice_fusion.7
  534.5 3.5 bitcast_dynamic-update-slice_fusion.7
  539.4 3.2 add_bitcast_fusion.2
  546.0 25.3 %while.78 = (s32[]{:T(128)}, f32[1,2,320,3072]{3,2,1,0:T(8,128)}, s32[2]{0:T(128)S(1)}, s32[2]{0:T(128)S(1)}, f32[2,2,256,256]{3,2,0,1:T(8,128)S(1)}, /*index=5*/s32[]{:T(128)}, s32[]{:T(128)}, s32[]{:T(128)}, s32[]{:T(128)}) while((s32[]{:T(128)}, f32[1,2,320,3072]{3,2,1,0:T(8,128)}, s32[2]{0:T(128)S(1)}, s32[2]{0:T(128)S(1)}, ...), condition=%wide.region_4.4_spmd, body=%wide.region_3.3_spmd.sunk | while | flops 131080 | bytes 2621649 | solution.py:106
  552.5 6.3 dynamic_update_slice.21
  565.2 6.2 dynamic_update_slice.21
  572.3 3.8 convert.14
  577.6 134.2 %collective-permute-start.9 = (bf16[1,2,64,3072]{3,2,1,0:T(8,128)(2,1)}, bf16[1,2,64,3072]{3,2,1,0:T(8,128)(2,1)S(1)}, u32[]{:S(2)}, u32[]{:S(2)}) collective-permute-start(bf16[1,2,64,3072]{3,2,1,0:T(8,128)(2,1)} %get-tuple-element.832), channel_id=1, source_target_pairs={{0,4},{1,5},{2,6},{3,7},{4,8},{5,9},{6,10},{7,11},{8,12},{9,13},{1... | collective-permute-start | bytes 2359304 | tf_op jit(solution)/shard_map/ppermute | solution.py:13
  711.8 3.6 collective-permute-start.8
  715.4 470.8 %all-reduce.1 = bf16[2,256,256]{2,1,0:T(8,128)(2,1)} all-reduce(f32[2,256,256]{2,1,0:T(8,128)S(1)} %copy-done.5), channel_id=1, replica_groups=mesh['depth'=4,'scan'=64] {'scan'}, use_global_device_ids=true, to_apply=%region_7.8 | all-reduce | flops 131072 | bytes 786432 | tf_op jit(solution)/shard_map/psum | solution.py:186
  1186.2 49.6 %reduce-scatter.2.cloned.1.call-done = bf16[2,64,256]{2,1,0:T(8,128)(2,1)} async-done(((bf16[2,256,256]{2,1,0:T(8,128)(2,1)}), bf16[2,64,256]{2,1,0:T(8,128)(2,1)}) %reduce-scatter.2.cloned.1.call-update) | async-done | bytes 65552 | tf_op jit(solution)/shard_map/reduce_scatter | solution.py:187
  1237.4 3.6 convert_add_fusion
  (363 shorter events, 228.4 us)
Async XLA Ops:
  7.2 1228.7 %reduce-scatter.2.cloned.1.call-start = ((), (), s32[]{:S(2)}) async-start(), calls=%async_computation.1 | async-start | bytes 327680 | tf_op jit(solution)/shard_map/reduce_scatter | solution.py:187
  7.2 108.3 %collective-permute-start.4 = (f32[1,2,64,3072]{3,2,1,0:T(8,128)}, f32[1,2,64,3072]{3,2,1,0:T(8,128)}, u32[]{:S(2)}, u32[]{:S(2)}) collective-permute-start(f32[1,2,64,3072]{3,2,1,0:T(8,128)} %param.11), channel_id=1, source_target_pairs={{0,61},{1,62},{2,63},{3,0},{4,1},{5,2},{6,3},{7,4},{8,5},{9,6},{10... | collective-permute-start | bytes 4718600 | tf_op jit(solution)/shard_map/ppermute | solution.py:13
  8.8 105.1 %collective-permute-start.3 = (f32[1,2,64,3072]{3,2,1,0:T(8,128)}, f32[1,2,64,3072]{3,2,1,0:T(8,128)}, u32[]{:S(2)}, u32[]{:S(2)}) collective-permute-start(f32[1,2,64,3072]{3,2,1,0:T(8,128)} %param.11), channel_id=1, source_target_pairs={{0,62},{1,63},{2,0},{3,1},{4,2},{5,3},{6,4},{7,5},{8,6},{9,7},{10,... | collective-permute-start | bytes 4718600 | tf_op jit(solution)/shard_map/ppermute | solution.py:13
  11.7 100.7 %collective-permute-start.2 = (f32[1,2,64,3072]{3,2,1,0:T(8,128)}, f32[1,2,64,3072]{3,2,1,0:T(8,128)}, u32[]{:S(2)}, u32[]{:S(2)}) collective-permute-start(f32[1,2,64,3072]{3,2,1,0:T(8,128)} %param.11), channel_id=1, source_target_pairs={{0,63},{1,0},{2,1},{3,2},{4,3},{5,4},{6,5},{7,6},{8,7},{9,8},{10,9... | collective-permute-start | bytes 4718600 | tf_op jit(solution)/shard_map/ppermute | solution.py:13
  13.1 133.9 %collective-permute-start.5 = (f32[1,2,64,3072]{3,2,1,0:T(8,128)}, f32[1,2,64,3072]{3,2,1,0:T(8,128)}, u32[]{:S(2)}, u32[]{:S(2)}) collective-permute-start(f32[1,2,64,3072]{3,2,1,0:T(8,128)} %param.11), channel_id=1, source_target_pairs={{0,60},{1,61},{2,62},{3,63},{4,0},{5,1},{6,2},{7,3},{8,4},{9,5},{1... | collective-permute-start | bytes 4718600 | tf_op jit(solution)/shard_map/ppermute | solution.py:13
  24.5 2.9 copy-start.8
  24.5 3.0 copy-start.6
  148.5 3.7 copy-start
  148.5 3.7 copy-start.7
  170.8 2.8 collective-permute-start.1
  192.2 10.7 collective-permute-start.1
  221.5 10.5 collective-permute-start.1
  250.7 10.5 collective-permute-start.1
  279.8 10.5 collective-permute-start.1
  316.2 1.2 copy-start.1
  316.2 1.4 copy-start.2
  321.6 28.2 %collective-permute-start = (bf16[2,2,256,256]{3,2,0,1:T(8,128)(2,1)}, bf16[2,2,256,256]{3,2,0,1:T(8,128)(2,1)}, u32[]{:S(2)}, u32[]{:S(2)}) collective-permute-start(bf16[2,2,256,256]{3,2,0,1:T(8,128)(2,1)} %fusion.198), channel_id=1, source_target_pairs={{64,0},{128,64},{192,128},{65,1},{129,65},{193,129},{66,2},{130,66... | collective-permute-start | bytes 1572872 | tf_op jit(solution)/shard_map/while/body/eval_jaxpr/ppermute | solution.py:19
  324.2 25.5 %copy-start.3 = (f32[2,256,256]{2,1,0:T(8,128)S(1)}, f32[2,256,256]{2,1,0:T(8,128)}, u32[]{:S(2)}) copy-start(f32[2,256,256]{2,1,0:T(8,128)} %get-tuple-element.1269) | copy-start | bytes 1572868 | tf_op jit(solution)/shard_map/while
  349.8 0.8 copy-start.4
  371.6 1.2 copy-start.1
  371.6 1.4 copy-start.2
  377.1 28.2 %collective-permute-start = (bf16[2,2,256,256]{3,2,0,1:T(8,128)(2,1)}, bf16[2,2,256,256]{3,2,0,1:T(8,128)(2,1)}, u32[]{:S(2)}, u32[]{:S(2)}) collective-permute-start(bf16[2,2,256,256]{3,2,0,1:T(8,128)(2,1)} %fusion.198), channel_id=1, source_target_pairs={{64,0},{128,64},{192,128},{65,1},{129,65},{193,129},{66,2},{130,66... | collective-permute-start | bytes 1572872 | tf_op jit(solution)/shard_map/while/body/eval_jaxpr/ppermute | solution.py:19
  379.6 25.5 %copy-start.3 = (f32[2,256,256]{2,1,0:T(8,128)S(1)}, f32[2,256,256]{2,1,0:T(8,128)}, u32[]{:S(2)}) copy-start(f32[2,256,256]{2,1,0:T(8,128)} %get-tuple-element.1269) | copy-start | bytes 1572868 | tf_op jit(solution)/shard_map/while
  405.3 0.8 copy-start.4
  427.1 1.2 copy-start.1
  427.1 1.4 copy-start.2
  432.5 28.2 %collective-permute-start = (bf16[2,2,256,256]{3,2,0,1:T(8,128)(2,1)}, bf16[2,2,256,256]{3,2,0,1:T(8,128)(2,1)}, u32[]{:S(2)}, u32[]{:S(2)}) collective-permute-start(bf16[2,2,256,256]{3,2,0,1:T(8,128)(2,1)} %fusion.198), channel_id=1, source_target_pairs={{64,0},{128,64},{192,128},{65,1},{129,65},{193,129},{66,2},{130,66... | collective-permute-start | bytes 1572872 | tf_op jit(solution)/shard_map/while/body/eval_jaxpr/ppermute | solution.py:19
  435.1 25.5 %copy-start.3 = (f32[2,256,256]{2,1,0:T(8,128)S(1)}, f32[2,256,256]{2,1,0:T(8,128)}, u32[]{:S(2)}) copy-start(f32[2,256,256]{2,1,0:T(8,128)} %get-tuple-element.1269) | copy-start | bytes 1572868 | tf_op jit(solution)/shard_map/while
  460.7 0.8 copy-start.4
  482.5 1.2 copy-start.1
  482.5 1.4 copy-start.2
  488.0 28.2 %collective-permute-start = (bf16[2,2,256,256]{3,2,0,1:T(8,128)(2,1)}, bf16[2,2,256,256]{3,2,0,1:T(8,128)(2,1)}, u32[]{:S(2)}, u32[]{:S(2)}) collective-permute-start(bf16[2,2,256,256]{3,2,0,1:T(8,128)(2,1)} %fusion.198), channel_id=1, source_target_pairs={{64,0},{128,64},{192,128},{65,1},{129,65},{193,129},{66,2},{130,66... | collective-permute-start | bytes 1572872 | tf_op jit(solution)/shard_map/while/body/eval_jaxpr/ppermute | solution.py:19
  490.5 25.5 %copy-start.3 = (f32[2,256,256]{2,1,0:T(8,128)S(1)}, f32[2,256,256]{2,1,0:T(8,128)}, u32[]{:S(2)}) copy-start(f32[2,256,256]{2,1,0:T(8,128)} %get-tuple-element.1269) | copy-start | bytes 1572868 | tf_op jit(solution)/shard_map/while
  516.2 0.8 copy-start.4
  538.0 1.2 copy-start.1
  538.0 1.4 copy-start.2
  543.4 28.1 %collective-permute-start = (bf16[2,2,256,256]{3,2,0,1:T(8,128)(2,1)}, bf16[2,2,256,256]{3,2,0,1:T(8,128)(2,1)}, u32[]{:S(2)}, u32[]{:S(2)}) collective-permute-start(bf16[2,2,256,256]{3,2,0,1:T(8,128)(2,1)} %fusion.198), channel_id=1, source_target_pairs={{64,0},{128,64},{192,128},{65,1},{129,65},{193,129},{66,2},{130,66... | collective-permute-start | bytes 1572872 | tf_op jit(solution)/shard_map/while/body/eval_jaxpr/ppermute | solution.py:19
  546.0 25.4 %copy-start.3 = (f32[2,256,256]{2,1,0:T(8,128)S(1)}, f32[2,256,256]{2,1,0:T(8,128)}, u32[]{:S(2)}) copy-start(f32[2,256,256]{2,1,0:T(8,128)} %get-tuple-element.1269) | copy-start | bytes 1572868 | tf_op jit(solution)/shard_map/while
  571.5 0.8 copy-start.4
  576.2 139.2 %copy-start.5 = (f32[2,256,256]{2,1,0:T(8,128)S(1)}, f32[2,256,256]{2,1,0:T(8,128)}, u32[]{:S(2)}) copy-start(f32[2,256,256]{2,1,0:T(8,128)} %get-tuple-element.618) | copy-start | bytes 1572868
  577.6 659.7 %collective-permute-start.6 = (bf16[1,2,64,3072]{3,2,1,0:T(8,128)(2,1)}, bf16[1,2,64,3072]{3,2,1,0:T(8,128)(2,1)S(1)}, u32[]{:S(2)}, u32[]{:S(2)}) collective-permute-start(bf16[1,2,64,3072]{3,2,1,0:T(8,128)(2,1)} %get-tuple-element.831), channel_id=1, source_target_pairs={{0,1},{1,2},{2,3},{3,4},{4,5},{5,6},{6,7},{7,8},{8,9},{9,10},{10,1... | collective-permute-start | bytes 2359304 | tf_op jit(solution)/shard_map/ppermute | solution.py:13
  577.6 659.7 %collective-permute-start.9 = (bf16[1,2,64,3072]{3,2,1,0:T(8,128)(2,1)}, bf16[1,2,64,3072]{3,2,1,0:T(8,128)(2,1)S(1)}, u32[]{:S(2)}, u32[]{:S(2)}) collective-permute-start(bf16[1,2,64,3072]{3,2,1,0:T(8,128)(2,1)} %get-tuple-element.832), channel_id=1, source_target_pairs={{0,4},{1,5},{2,6},{3,7},{4,8},{5,9},{6,10},{7,11},{8,12},{9,13},{1... | collective-permute-start | bytes 2359304 | tf_op jit(solution)/shard_map/ppermute | solution.py:13
  711.8 525.5 %collective-permute-start.8 = (bf16[1,2,64,3072]{3,2,1,0:T(8,128)(2,1)}, bf16[1,2,64,3072]{3,2,1,0:T(8,128)(2,1)}, u32[]{:S(2)}, u32[]{:S(2)}) collective-permute-start(bf16[1,2,64,3072]{3,2,1,0:T(8,128)(2,1)} %get-tuple-element.833), channel_id=1, source_target_pairs={{0,3},{1,4},{2,5},{3,6},{4,7},{5,8},{6,9},{7,10},{8,11},{9,12},{10... | collective-permute-start | bytes 2359304 | tf_op jit(solution)/shard_map/ppermute | solution.py:13
  715.4 521.9 %collective-permute-start.7 = (bf16[1,2,64,3072]{3,2,1,0:T(8,128)(2,1)S(1)}, bf16[1,2,64,3072]{3,2,1,0:T(8,128)(2,1)}, u32[]{:S(2)}, u32[]{:S(2)}) collective-permute-start(bf16[1,2,64,3072]{3,2,1,0:T(8,128)(2,1)S(1)} %get-tuple-element.834), channel_id=1, source_target_pairs={{0,2},{1,3},{2,4},{3,5},{4,6},{5,7},{6,8},{7,9},{8,10},{9,11},{10,... | collective-permute-start | bytes 2359304 | tf_op jit(solution)/shard_map/ppermute | solution.py:13
Sparse Core Ops, SparseCore 0:
  1186.3 49.4 reduce-scatter.1
where the time goes:
time: 1260 us; the launch traced here: 1250 us
  blocking collectives  471 us (37%)
  local copies, waits for them, and re-layouts  209 us (17%)
  starting transfers between devices  196 us (16%)
  waiting for transfers between devices  172 us (14%)
  matrix products  93.7 us (7%)
  other arithmetic  51.7 us (4%)
  loops' own time  40.9 us (3%)
  between operations  14.2 us (1%)
    psum x1, blocking collectives, local(): partial_total = lax.psum(probe_total, 'scan')  471 us
    ppermute x8, starting transfers between devices, from_behind(): lax.ppermute(value, axis, [(i, (i + by) % length) for i in range(length)])  152 us
    ppermute x8, waiting for transfers between devices, from_behind(): lax.ppermute(value, axis, [(i, (i + by) % length) for i in range(length)])  115 us
    gather x60, local copies, waits for them, and re-layouts  74.9 us
    dynamic_update_slice x10, local copies, waits for them, and re-layouts, place(): lax.dynamic_update_slice(buffer_now, before + pieces[position][None], anc...  62.8 us
    dot_general x40, matrix products, apply_right(): jnp.einsum('kab,nb->kan', values, matrix, precision=lax.Precision.HIGHEST...  55.6 us
    reduce_scatter x1, waiting for transfers between devices, local(): lax.psum_scatter(partial_total.astype(jnp.bfloat16), 'depth', scatter_dim...  49.6 us
    ppermute x10, starting transfers between devices, shifted(): return lax.ppermute(block, axis, route)  43.9 us
  transfers between devices with their start and end apart: 19, of which 8 were waited for; matrix products, arithmetic and copies ran while one was open for 9% of the time, Pallas kernels for 0%

commit v1 on v0

v1 whole, which is shorter than its diff:
```python
import functools
import math

import jax
import jax.numpy as jnp
import numpy as np
from jax import lax
from jax.experimental import pallas as pl
from jax.experimental.pallas import tpu as pltpu
from jax.sharding import PartitionSpec as P

FRESNEL = 0.25
SIDE = 256
HALF = SIDE // 2
STRIP = 64
RIM = SIDE // STRIP
BATCHES = 2
PER = 2
F32 = jnp.float32
BF16 = jnp.bfloat16
MESH = pl.DeviceIdType.MESH


def tables():
    k = np.arange(SIDE)
    f = np.where(k < HALF, k, k - SIDE).astype(np.float64)
    h = np.exp(-1j * math.pi * FRESNEL * f * f / SIDE)
    dft = np.exp(-2j * math.pi * (np.outer(k, k) % SIDE) / SIDE)
    a = (dft.conj() / SIDE) @ (h[:, None] * dft)
    lefts, rights = [], []
    for sign in (1.0, -1.0):
        m = (a[:HALF, :HALF] + sign * a[:HALF, HALF:]) / 2.0
        left = np.block([[m.real, -m.imag], [m.imag, m.real]]).astype(np.float32)
        for out, full in ((lefts, left), (rights, left.T.copy())):
            high = full.astype(jnp.bfloat16)
            low = (full - high.astype(np.float32)).astype(jnp.bfloat16)
            out.append(np.stack([high, low]))
    return np.stack([np.stack(lefts), np.stack(rights)])


def dot(a, b):
    return jnp.dot(a, b, preferred_element_type=F32)


def split(x):
    high = x.astype(BF16)
    return high, (x - high.astype(F32)).astype(BF16)


def propagate(x_ref, w_ref, tab):
    middle = []
    for a in range(2):
        parts = []
        for ri in range(2):
            top, low = x_ref[ri, :HALF, :], x_ref[ri, HALF:, :]
            v = top + low if a == 0 else top - low
            l, r = v[:, :HALF], v[:, HALF:]
            parts.append(jnp.concatenate([l + r, l - r], axis=1))
        high, low = split(jnp.concatenate(parts, axis=0))
        left_high, left_low = tab[0, a, 0], tab[0, a, 1]
        middle.append(dot(left_high, high) + dot(left_low, high) + dot(left_high, low))
    sectors = []
    for b in range(2):
        cols = slice(b * HALF, (b + 1) * HALF)
        rows = [jnp.concatenate([z[:HALF, cols], z[HALF:, cols]], axis=1) for z in middle]
        high, low = split(jnp.concatenate(rows, axis=0))
        right_high, right_low = tab[1, b, 0], tab[1, b, 1]
        sectors.append(dot(high, right_high) + dot(high, right_low) + dot(low, right_high))
    for ri in range(2):
        cols = slice(ri * HALF, (ri + 1) * HALF)
        for half_col in range(2):
            s, d = sectors[0][:, cols], sectors[1][:, cols]
            v = s + d if half_col == 0 else s - d
            out = slice(half_col * HALF, (half_col + 1) * HALF)
            w_ref[ri, :HALF, out] = v[:HALF] + v[HALF:]
            w_ref[ri, HALF:, out] = v[:HALF] - v[HALF:]


def times(ar, ai, br, bi):
    return ar * br - ai * bi, ar * bi + ai * br


def main_kernel(
    group, hi_count, n_scan,
    trans, probe, exit_adjoint, table_in, idx_in,
    pieces, idx_all, probe_out,
    strip, tab, probe_v, exit_v, idx_s,
    sbuf, tbuf, x_v, start_v, w1_v, w2_v, w3_v, w4_v, zsend, zrecv,
    gbuf, total_v, part_s, part_r, rs_s, rs_r, ar_s, ar_r,
    local_sems, strip_sems, idx_send, idx_recv, t_send, t_recv, z_send, z_recv,
    g_send, g_recv, p_send, p_recv, rs_send, rs_recv, ar_send, ar_recv, ag_send, ag_recv,
):
    q = lax.axis_index("depth")
    j = lax.axis_index("scan")
    z = q // 2
    c = q % 2
    member = j % group
    level = j // group

    def at(depth, scan):
        return {"depth": depth, "scan": scan}

    def region(step):
        return lax.rem(j + step + n_scan, n_scan)

    def mate(i):
        return level * group + lax.rem(member + i, group)

    def tier(i):
        return lax.rem(level + i, hi_count) * group + member

    loads = [
        pltpu.make_async_copy(table_in, tab, local_sems.at[1]),
        pltpu.make_async_copy(probe, probe_v, local_sems.at[2]),
        pltpu.make_async_copy(exit_adjoint.at[c], exit_v, local_sems.at[3]),
        pltpu.make_async_copy(idx_in, idx_all.at[0], local_sems.at[4]),
    ]

    def strip_copy(i):
        cols = pl.ds(pl.multiple_of(i * HALF, HALF), HALF)
        return pltpu.make_async_copy(trans.at[0, :, :, cols], strip.at[i], strip_sems.at[i])

    for copy in loads:
        copy.start()

    def start_strip(i, carry):
        strip_copy(i).start()
        return carry

    def wait_strip(i, carry):
        strip_copy(i).wait()
        return carry

    lax.fori_loop(0, strip.shape[0], start_strip, 0)

    barrier = pltpu.get_barrier_semaphore()
    partners = [at(q + 1 - 2 * c, j), at(q + 2 - 4 * z, j), at(3 - q, j)]
    for d in range(1, RIM + 1):
        for b in range(2):
            partners.append(at(2 * z + b, region(d)))
            partners.append(at(2 * z + b, region(-d)))
    for i in range(1, group):
        partners.append(at(q, mate(i)))
    for i in range(1, hi_count):
        partners.append(at(q, tier(i)))
    for device in partners:
        pl.semaphore_signal(barrier, inc=1, device_id=device, device_id_type=MESH)
    pl.semaphore_wait(barrier, len(partners))

    idx_copies = [
        pltpu.make_async_remote_copy(
            src_ref=idx_in, dst_ref=idx_all.at[d], send_sem=idx_send.at[d], recv_sem=idx_recv.at[d],
            device_id=at(q, region(d)), device_id_type=MESH)
        for d in range(1, RIM + 1)
    ]
    for copy in idx_copies:
        copy.start()
    loads[3].wait()
    for copy in idx_copies:
        copy.wait_recv()
    to_smem = pltpu.make_async_copy(idx_all, idx_s, local_sems.at[5])
    to_smem.start()
    to_smem.wait()
    lax.fori_loop(0, strip.shape[0], wait_strip, 0)

    lane = lax.broadcasted_iota(jnp.int32, (1, 1, HALF), 2)
    last_block = strip.shape[0] - 1

    def t_copy(k, d, b):
        return pltpu.make_async_remote_copy(
            src_ref=sbuf.at[k, d, b], dst_ref=tbuf.at[k, c, d],
            send_sem=t_send.at[k, d, b], recv_sem=t_recv.at[k, c, d],
            device_id=at(2 * z + b, region(-d)), device_id_type=MESH)

    def t_sibling(k):
        return pltpu.make_async_remote_copy(
            src_ref=sbuf.at[k, 0, 1 - c], dst_ref=tbuf.at[k, c, 0],
            send_sem=t_send.at[k, 0, 1], recv_sem=t_recv.at[k, c, 0],
            device_id=at(q + 1 - 2 * c, j), device_id_type=MESH)

    def t_local(k):
        return pltpu.make_async_copy(sbuf.at[k, 0, c], tbuf.at[k, c, 0], t_send.at[k, 0, 0])

    def t_arrival(k, slot, d):
        return pltpu.make_async_remote_copy(
            src_ref=sbuf.at[k, d, 0], dst_ref=tbuf.at[k, slot, d],
            send_sem=t_send.at[k, d, 0], recv_sem=t_recv.at[k, slot, d],
            device_id=at(q + 1 - 2 * c, j), device_id_type=MESH)

    def send_windows(k, carry):
        for d in (4, 3, 2, 1, 0):
            for b in range(2):
                col = idx_s[d, 0, 4 + 2 * b + k]
                block = lax.shift_right_logical(col, 7)
                offset = col & (HALF - 1)
                first, second = strip[block], strip[block + 1]
                third = strip[jnp.minimum(block + 2, last_block)]
                sbuf[k, d, b, :, :, :HALF] = jnp.where(lane >= offset, first, third).astype(BF16)
                sbuf[k, d, b, :, :, HALF:] = second.astype(BF16)
                if d > 0:
                    t_copy(k, d, b).start()
        t_sibling(k).start()
        t_local(k).start()
        return carry

    lax.fori_loop(0, PER, send_windows, 0)

    def wait_windows(k):
        for d in (0, 1, 2, 3, 4):
            if d == 0:
                t_local(k).wait()
                t_arrival(k, 1 - c, 0).wait_recv()
            else:
                for slot in range(2):
                    t_arrival(k, slot, d).wait_recv()

    row = lax.broadcasted_iota(jnp.int32, (STRIP, 1), 0)

    def offsets(k):
        e = 2 * c + k
        return idx_s[0, 0, e] & (STRIP - 1), idx_s[0, 0, 4 + e] & (HALF - 1)

    def window(k, slot, block, row_offset):
        if block > 0:
            return tbuf[k, slot, block, 0].astype(F32), tbuf[k, slot, block, 1].astype(F32)
        here = row >= row_offset
        return tuple(
            jnp.where(here, tbuf[k, slot, 0, ri].astype(F32), tbuf[k, slot, RIM, ri].astype(F32))
            for ri in range(2)
        )

    blocks = [slice(i * STRIP, (i + 1) * STRIP) for i in range(RIM)]

    def roll(x, rows, cols):
        return pltpu.roll(pltpu.roll(x, rows, 0), cols, 1)

    def z_copy(k):
        return pltpu.make_async_remote_copy(
            src_ref=zsend.at[k], dst_ref=zrecv.at[k], send_sem=z_send.at[k], recv_sem=z_recv.at[k],
            device_id=at(q + 2 - 4 * z, j), device_id_type=MESH)

    for copy in loads[:3]:
        copy.wait()

    def first_half(k, carry):
        row_offset, col_offset = offsets(k)

        @pl.when(z == 0)
        def _():
            for ri in range(2):
                start_v[k, ri] = roll(probe_v[ri], row_offset, col_offset)
            wait_windows(k)
            for i, rows in enumerate(blocks):
                tr, ti = window(k, 0, i, row_offset)
                x_v[0, rows, :], x_v[1, rows, :] = times(tr, ti, start_v[k, 0, rows, :], start_v[k, 1, rows, :])

        @pl.when(z == 1)
        def _():
            x_v[0] = roll(exit_v[k, 0], row_offset, col_offset)
            x_v[1] = -roll(exit_v[k, 1], row_offset, col_offset)

        propagate(x_v, w1_v.at[k], tab)

        @pl.when(z == 1)
        def _():
            wait_windows(k)

        for i, rows in enumerate(blocks):
            tr, ti = window(k, 1, i, row_offset)
            x_v[0, rows, :], x_v[1, rows, :] = times(tr, ti, w1_v[k, 0, rows, :], w1_v[k, 1, rows, :])
        propagate(x_v, w2_v.at[k], tab)

        @pl.when(z == 0)
        def _():
            zsend[k] = w2_v[k].astype(BF16)

        @pl.when(z == 1)
        def _():
            for i, rows in enumerate(blocks):
                tr, ti = window(k, 0, i, row_offset)
                vr, vi = times(tr, ti, w2_v[k, 0, rows, :], w2_v[k, 1, rows, :])
                zsend[k, 0, rows, :] = vr.astype(BF16)
                zsend[k, 1, rows, :] = vi.astype(BF16)

        z_copy(k).start()
        return carry

    lax.fori_loop(0, PER, first_half, 0)

    def g_copy(k, slot, d):
        return pltpu.make_async_remote_copy(
            src_ref=gbuf.at[k, slot, d % RIM], dst_ref=pieces.at[k, c, d],
            send_sem=g_send.at[k, slot, d], recv_sem=g_recv.at[k, c, d],
            device_id=at(2 * z + slot, region(d)), device_id_type=MESH)

    def g_sibling(k):
        return pltpu.make_async_remote_copy(
            src_ref=gbuf.at[k, 1 - c, 0], dst_ref=pieces.at[k, c, 0],
            send_sem=g_send.at[k, 1, 0], recv_sem=g_recv.at[k, c, 0],
            device_id=at(q + 1 - 2 * c, j), device_id_type=MESH)

    def g_local(k):
        return pltpu.make_async_copy(gbuf.at[k, c, 0], pieces.at[k, c, 0], g_send.at[k, 0, 0])

    def g_arrival(k, core, d):
        return pltpu.make_async_remote_copy(
            src_ref=gbuf.at[k, 0, d % RIM], dst_ref=pieces.at[k, core, d],
            send_sem=g_send.at[k, 0, d], recv_sem=g_recv.at[k, core, d],
            device_id=at(q + 1 - 2 * c, j), device_id_type=MESH)

    def second_half(k, carry):
        row_offset, col_offset = offsets(k)
        z_copy(k).wait_recv()

        @pl.when(z == 0)
        def _():
            x_v[...] = zrecv[k].astype(F32)

        @pl.when(z == 1)
        def _():
            for i, rows in enumerate(blocks):
                tr, ti = window(k, 0, i, row_offset)
                vr, vi = zrecv[k, 0, rows, :].astype(F32), zrecv[k, 1, rows, :].astype(F32)
                x_v[0, rows, :], x_v[1, rows, :] = times(tr, ti, vr, vi)
                gr, gi = times(vr, vi, w2_v[k, 0, rows, :], w2_v[k, 1, rows, :])
                gbuf[k, 0, i, 0] = gr.astype(BF16)
                gbuf[k, 0, i, 1] = (-gi).astype(BF16)

        propagate(x_v, w3_v, tab)
        for i, rows in enumerate(blocks):
            gr, gi = times(w1_v[k, 0, rows, :], w1_v[k, 1, rows, :], w3_v[0, rows, :], w3_v[1, rows, :])
            gbuf[k, 1, i, 0] = gr.astype(BF16)
            gbuf[k, 1, i, 1] = (-gi).astype(BF16)
        for d in (4, 3, 2, 1):
            g_copy(k, 1, d).start()

        @pl.when(z == 0)
        def _():
            for i, rows in enumerate(blocks):
                tr, ti = window(k, 1, i, row_offset)
                x_v[0, rows, :], x_v[1, rows, :] = times(tr, ti, w3_v[0, rows, :], w3_v[1, rows, :])
            propagate(x_v, w4_v, tab)
            for i, rows in enumerate(blocks):
                wr, wi = w4_v[0, rows, :], w4_v[1, rows, :]
                gr, gi = times(start_v[k, 0, rows, :], start_v[k, 1, rows, :], wr, wi)
                gbuf[k, 0, i, 0] = gr.astype(BF16)
                gbuf[k, 0, i, 1] = (-gi).astype(BF16)

        for d in (4, 3, 2, 1):
            g_copy(k, 0, d).start()
        g_sibling(k).start()
        g_local(k).start()

        @pl.when(z == 0)
        def _():
            for i, rows in enumerate(blocks):
                tr, ti = window(k, 0, i, row_offset)
                vr, vi = times(tr, ti, w4_v[0, rows, :], w4_v[1, rows, :])
                x_v[0, rows, :], x_v[1, rows, :] = vr, -vi
            back_rows, back_cols = (SIDE - row_offset) & (SIDE - 1), (SIDE - col_offset) & (SIDE - 1)
            for ri in range(2):
                moved = roll(x_v[ri], back_rows, back_cols)
                total_v[ri] = jnp.where(k > 0, total_v[ri], 0.0) + moved

        return carry

    lax.fori_loop(0, PER, second_half, 0)

    def p_copy(section):
        return pltpu.make_async_remote_copy(
            src_ref=part_s.at[section], dst_ref=part_r.at[c], send_sem=p_send.at[section],
            recv_sem=p_recv.at[c], device_id=at(section, j), device_id_type=MESH)

    def p_arrival(core):
        return pltpu.make_async_remote_copy(
            src_ref=part_s.at[0], dst_ref=part_r.at[core], send_sem=p_send.at[0],
            recv_sem=p_recv.at[core], device_id=at(q + 1 - 2 * c, j), device_id_type=MESH)

    @pl.when(z == 0)
    def _():
        for section in range(4):
            part_s[section] = total_v[:, section * STRIP:(section + 1) * STRIP, :].astype(BF16)
        p_copy(2).start()
        p_copy(3).start()
        p_copy(1 - c).start()
        own = pltpu.make_async_copy(part_s.at[c], part_r.at[c], p_send.at[c])
        own.start()
        own.wait()
        p_arrival(1 - c).wait_recv()

    @pl.when(z == 1)
    def _():
        p_arrival(0).wait_recv()
        p_arrival(1).wait_recv()

    block_sum = part_r[0].astype(F32) + part_r[1].astype(F32)
    rs_s[...] = block_sum.reshape(rs_s.shape)

    def rs_copy(i):
        target = lax.rem(member + i, group)
        return pltpu.make_async_remote_copy(
            src_ref=rs_s.at[target], dst_ref=rs_r.at[member], send_sem=rs_send.at[i],
            recv_sem=rs_recv.at[i], device_id=at(q, mate(i)), device_id_type=MESH)

    for i in range(1, group):
        rs_copy(i).start()
    rs_r[member] = rs_s[member]
    for i in range(1, group):
        rs_copy(i).wait_recv()
    piece_sum = rs_r[0]
    for m in range(1, group):
        piece_sum = piece_sum + rs_r[m]
    ar_s[...] = piece_sum
    ar_r[level] = piece_sum

    def ar_copy(i):
        return pltpu.make_async_remote_copy(
            src_ref=ar_s, dst_ref=ar_r.at[level], send_sem=ar_send.at[i],
            recv_sem=ar_recv.at[i], device_id=at(q, tier(i)), device_id_type=MESH)

    for i in range(1, hi_count):
        ar_copy(i).start()
    for i in range(1, hi_count):
        ar_copy(i).wait()
    piece_sum = ar_r[0]
    for m in range(1, hi_count):
        piece_sum = piece_sum + ar_r[m]
    probe_out[member] = piece_sum

    def ag_copy(i):
        return pltpu.make_async_remote_copy(
            src_ref=probe_out.at[member], dst_ref=probe_out.at[member], send_sem=ag_send.at[i],
            recv_sem=ag_recv.at[i], device_id=at(q, mate(i)), device_id_type=MESH)

    for i in range(1, group):
        ag_copy(i).start()
    for i in range(1, group):
        ag_copy(i).wait()

    for copy in idx_copies:
        copy.wait_send()
    for i in range(1, group):
        rs_copy(i).wait_send()

    @pl.when(z == 0)
    def _():
        p_copy(2).wait_send()
        p_copy(3).wait_send()
        p_copy(1 - c).wait_send()

    def drain(k, carry):
        z_copy(k).wait_send()
        t_sibling(k).wait_send()
        g_sibling(k).wait_send()
        g_local(k).wait()
        g_arrival(k, 1 - c, 0).wait_recv()
        for d in range(1, RIM + 1):
            for b in range(2):
                t_copy(k, d, b).wait_send()
                g_copy(k, b, d).wait_send()
                g_arrival(k, b, d).wait_recv()
        return carry

    lax.fori_loop(0, PER, drain, 0)


def main_call(transmission, probe, exit_adjoint, idx):
    n_scan = lax.axis_size("scan")
    group = 16 if n_scan % 16 == 0 else 4
    hi_count = n_scan // group
    piece = (16 // group, 8, SIDE)
    any_spec = pl.BlockSpec(memory_space=pl.ANY)
    vmem_spec = pl.BlockSpec(memory_space=pltpu.VMEM)
    field = (2, SIDE, SIDE)
    dma = pltpu.SemaphoreType.DMA
    columns = transmission.shape[3]
    return pl.pallas_call(
        functools.partial(main_kernel, group, hi_count, n_scan),
        out_shape=(
            jax.ShapeDtypeStruct((PER, 2, RIM + 1, 2, STRIP, SIDE), BF16),
            jax.ShapeDtypeStruct((RIM + 1, 8, 128), jnp.int32),
            jax.ShapeDtypeStruct((group,) + piece, F32),
        ),
        in_specs=[any_spec] * 5,
        out_specs=(any_spec, any_spec, vmem_spec),
        scratch_shapes=[
            pltpu.VMEM((columns // HALF, 2, STRIP, HALF), F32),
            pltpu.VMEM((2, 2, 2, SIDE, SIDE), BF16),
            pltpu.VMEM(field, F32),
            pltpu.VMEM((PER,) + field, F32),
            pltpu.SMEM((RIM + 1, 8, 128), jnp.int32),
            pltpu.VMEM((PER, RIM + 1, 2, 2, STRIP, SIDE), BF16),
            pltpu.VMEM((PER, 2, RIM + 1, 2, STRIP, SIDE), BF16),
            pltpu.VMEM(field, F32),
            pltpu.VMEM((PER,) + field, F32),
            pltpu.VMEM((PER,) + field, F32),
            pltpu.VMEM((PER,) + field, F32),
            pltpu.VMEM(field, F32),
            pltpu.VMEM(field, F32),
            pltpu.VMEM((PER,) + field, BF16),
            pltpu.VMEM((PER,) + field, BF16),
            pltpu.VMEM((PER, 2, RIM, 2, STRIP, SIDE), BF16),
            pltpu.VMEM(field, F32),
            pltpu.VMEM((4, 2, STRIP, SIDE), BF16),
            pltpu.VMEM((2, 2, STRIP, SIDE), BF16),
            pltpu.VMEM((group,) + piece, F32),
            pltpu.VMEM((group,) + piece, F32),
            pltpu.VMEM(piece, F32),
            pltpu.VMEM((hi_count,) + piece, F32),
            dma((6,)),
            dma((columns // HALF,)),
            dma((RIM + 1,)),
            dma((RIM + 1,)),
            dma((PER, RIM + 1, 2)),
            dma((PER, 2, RIM + 1)),
            dma((PER,)),
            dma((PER,)),
            dma((PER, 2, RIM + 1)),
            dma((PER, 2, RIM + 1)),
            dma((4,)),
            dma((2,)),
            dma((group,)),
            dma((group,)),
            dma((hi_count,)),
            dma((hi_count,)),
            dma((group,)),
            dma((group,)),
        ],
        compiler_params=pltpu.CompilerParams(
            collective_id=0, has_side_effects=True, vmem_limit_bytes=48 * 1024 * 1024
        ),
        cost_estimate=pl.CostEstimate(flops=8 * 12 * 2 * SIDE**3, bytes_accessed=8 << 20, transcendentals=0),
        name="waves",
    )(transmission, probe, exit_adjoint, jnp.asarray(tables()), idx)


def deposit_kernel(idx, pieces, probe_in, grad, probe_out):
    probe_out[...] = probe_in[...]
    grad[...] = jnp.zeros_like(grad)
    lane = lax.broadcasted_iota(jnp.int32, (1, 1, HALF), 2)
    row = lax.broadcasted_iota(jnp.int32, (1, STRIP, 1), 1)

    def add(n, carry):
        d = n // 4
        core = (n // 2) % 2
        k = n % 2
        e = 2 * core + k
        row_offset = idx[d, 0, e] & (STRIP - 1)
        col = idx[d, 0, 4 + e]
        block = lax.shift_right_logical(col, 7)
        col_offset = col & (HALF - 1)
        low = jnp.where(d == 0, row_offset, 0)
        high = jnp.where(d == RIM, row_offset, STRIP)
        keep = (row >= low) & (row < high)
        piece = jnp.where(keep, pieces[k, core, d].astype(F32), 0.0)
        first, second = piece[:, :, :HALF], piece[:, :, HALF:]
        here = lane >= col_offset
        third_block = jnp.minimum(block + 2, grad.shape[3] // HALF - 1)
        for where_to, value in (
            (block, jnp.where(here, first, 0.0)),
            (block + 1, second),
            (third_block, jnp.where(here, 0.0, first)),
        ):
            cols = pl.ds(pl.multiple_of(where_to * HALF, HALF), HALF)
            grad[0, :, :, cols] = grad[0, :, :, cols] + value
        return carry

    lax.fori_loop(0, 4 * (RIM + 1), add, 0)


def deposit_call(idx_all, pieces, probe_sum, columns):
    vmem_spec = pl.BlockSpec(memory_space=pltpu.VMEM)
    return pl.pallas_call(
        deposit_kernel,
        out_shape=(
            jax.ShapeDtypeStruct((1, 2, STRIP, columns), F32),
            jax.ShapeDtypeStruct(probe_sum.shape, F32),
        ),
        in_specs=[pl.BlockSpec(memory_space=pltpu.SMEM), vmem_spec, vmem_spec],
        out_specs=(vmem_spec, vmem_spec),
        compiler_params=pltpu.CompilerParams(vmem_limit_bytes=32 * 1024 * 1024),
        name="deposit",
    )(idx_all, pieces, probe_sum)


def local(transmission, probe, exit_adjoint, scan_row, scan_col):
    head = jnp.concatenate([scan_row.reshape(1, 4), scan_col.reshape(1, 4)], axis=1)
    idx = jnp.pad(head, ((0, 7), (0, 120)))
    pieces, idx_all, probe_sum = main_call(transmission, probe, exit_adjoint, idx)
    object_grad, probe_grad = deposit_call(idx_all, pieces, probe_sum, transmission.shape[3])
    return object_grad, probe_grad.reshape(2, STRIP, SIDE)


def solution(mesh):
    placed = (
        P("depth", None, "scan", None),
        P(),
        P(None, "scan", None, None, None),
        P(None, "scan"),
        P(None, "scan"),
    )
    return jax.shard_map(
        local,
        mesh=mesh,
        in_specs=placed,
        out_specs=(P("depth", None, "scan", None), P(None, "depth", None)),
        check_vma=False,
    )
```

time: 1260 us -> 145 us (0.12)
  the two profiles are of different devices: /device:TPU:4 before, /device:TPU:32 now
where the time goes in v1:
time: 145 us
  Pallas kernels  139 us (96%)
  local copies, waits for them, and re-layouts  5.2 us (4%)
    pallas_call x1, Pallas kernels, main_call(): pl.pallas_call(functools.partial(main_kernel, group, hi_count, n_scan), o...  136 us
    unnamed x6, local copies, waits for them, and re-layouts  3.67 us
    pallas_call x1, Pallas kernels, deposit_call(): pl.pallas_call(deposit_kernel, out_shape=(jax.ShapeDtypeStruct((1, 2, STR...  3.35 us

profile of v1, /device:TPU:32, one launch (start us, length us, event | category | flops | bytes accessed | tf_op | source)
XLA Modules:
  0.0 144.9 jit_solution(10499681842361664438)
XLA Ops:
  0.6 0.8 reshape.13
  1.4 0.8 reshape.14
  2.1 0.1 pad_add_fusion
  2.2 0.0 copy-start
  2.2 1.4 copy-done
  3.6 0.0 copy-start.1
  3.6 1.0 copy-done.1
  4.7 0.0 copy-start.2
  4.7 1.2 copy-done.2
  5.9 135.7 %waves.1 = (bf16[2,2,5,2,64,256]{5,4,3,2,1,0:T(8,128)(2,1)S(1)}, s32[5,8,128]{2,1,0:T(8,128)S(1)}, f32[16,1,8,256]{3,2,1,0:T(8,128)S(1)}) custom-call(f32[1,2,64,3072]{3,2,1,0:T(8,128)S(1)} %copy-done, f32[2,256,256]{2,1,0:T(8,128)S(1)} %copy-done.1, f32[2,2,2,256,256]{4,3,2,1,0:T(8,128)} %exit_adjoint.1, bf16[2,2,2,256,256]{4,3,2,1,0:T(8,128)(2,1)S(1)} %copy-done.2, ...), custom_call_target="tpu_custom_call" | custom-call | flops 3221225472 | bytes 8388608 | tf_op jit(solution)/shard_map/waves/pallas_call | solution.py:477
  141.6 3.3 %deposit.1 = (f32[1,2,64,3072]{3,2,1,0:T(8,128)}, f32[16,1,8,256]{3,2,1,0:T(8,128)}) custom-call(s32[5,8,128]{2,1,0:T(8,128)S(1)} %get-tuple-element.7.idx, bf16[2,2,5,2,64,256]{5,4,3,2,1,0:T(8,128)(2,1)S(1)} %get-tuple-element.8.pieces, f32[16,1,8,256]{3,2,1,0:T(8,128)S(1)} %get-tuple-element.9.probe_in), custom_call_target="tpu_custom_call" | custom-call | tf_op jit(solution)/shard_map/deposit/pallas_call | solution.py:573
  (1 shorter events, 0.0 us)
Async XLA Ops:
  2.2 1.4 copy-start
  3.6 1.0 copy-start.1
  4.7 1.2 copy-start.2

commit v2 on v1

--- a/solution.py
+++ b/solution.py
@@ -81,21 +81,25 @@
 
 
 def main_kernel(
-    group, hi_count, n_scan,
+    across, hi_count, n_scan,
     trans, probe, exit_adjoint, table_in, idx_in,
     pieces, idx_all, probe_out,
     strip, tab, probe_v, exit_v, idx_s,
     sbuf, tbuf, x_v, start_v, w1_v, w2_v, w3_v, w4_v, zsend, zrecv,
-    gbuf, total_v, part_s, part_r, rs_s, rs_r, ar_s, ar_r,
-    local_sems, strip_sems, idx_send, idx_recv, t_send, t_recv, z_send, z_recv,
-    g_send, g_recv, p_send, p_recv, rs_send, rs_recv, ar_send, ar_recv, ag_send, ag_recv,
+    t_transit, g_transit, gbuf, total_v, part_s, part_r, rs_s, rs_r, ar_s, ar_r,
+    local_sems, strip_sems, idx_send, idx_recv, t_send, t_recv, tt_send, tt_recv, z_send, z_recv,
+    g_send, g_recv, gt_send, gt_recv, p_send, p_recv, rs_send, rs_recv, ar_send, ar_recv, ag_send, ag_recv,
 ):
     q = lax.axis_index("depth")
     j = lax.axis_index("scan")
     z = q // 2
     c = q % 2
+    group = RIM * across
     member = j % group
     level = j // group
+    y = j % RIM
+    x = member // RIM
+    span = RIM * (across - 1)
 
     def at(depth, scan):
         return {"depth": depth, "scan": scan}
@@ -145,7 +149,14 @@
         partners.append(at(q, tier(i)))
     for device in partners:
         pl.semaphore_signal(barrier, inc=1, device_id=device, device_id_type=MESH)
-    pl.semaphore_wait(barrier, len(partners))
+    crossing = ((x == 0, span), (x == across - 1, -span))
+    for edge, step in crossing:
+        @pl.when(edge)
+        def _(step=step):
+            pl.semaphore_signal(
+                barrier, inc=1, device_id=at(q + 1 - 2 * c, region(step)), device_id_type=MESH)
+    on_edge = ((x == 0) | (x == across - 1)).astype(jnp.int32)
+    pl.semaphore_wait(barrier, len(partners) + on_edge)
 
     idx_copies = [
         pltpu.make_async_remote_copy(
@@ -166,11 +177,56 @@
     lane = lax.broadcasted_iota(jnp.int32, (1, 1, HALF), 2)
     last_block = strip.shape[0] - 1
 
-    def t_copy(k, d, b):
-        return pltpu.make_async_remote_copy(
-            src_ref=sbuf.at[k, d, b], dst_ref=tbuf.at[k, c, d],
-            send_sem=t_send.at[k, d, b], recv_sem=t_recv.at[k, c, d],
-            device_id=at(2 * z + b, region(-d)), device_id_type=MESH)
+    def t_copy(k, d, b, target, buffer=None):
+        return pltpu.make_async_remote_copy(
+            src_ref=sbuf.at[k, d, b], dst_ref=tbuf.at[k, c, d] if buffer is None else buffer,
+            send_sem=t_send.at[k, d, b],
+            recv_sem=t_recv.at[k, c, d] if buffer is None else tt_recv.at[k, d - 1 + c * (d // RIM)],
+            device_id=at(2 * z + b, target), device_id_type=MESH)
+
+    def t_start(k, d, b):
+        if d == RIM:
+            @pl.when(x == 0)
+            def _():
+                t_copy(k, d, b, region(span), t_transit.at[k, d - 1 + c]).start()
+
+            @pl.when(x > 0)
+            def _():
+                t_copy(k, d, b, region(-d)).start()
+            return
+
+        turned = (y < d) & (c == b)
+
+        @pl.when(turned)
+        def _():
+            t_copy(k, d, b, region(RIM - d), t_transit.at[k, d - 1]).start()
+
+        @pl.when(jnp.logical_not(turned))
+        def _():
+            t_copy(k, d, b, region(-d)).start()
+
+    def t_onward(k, slot, d, entry, step):
+        return pltpu.make_async_remote_copy(
+            src_ref=t_transit.at[k, entry], dst_ref=tbuf.at[k, slot, d],
+            send_sem=tt_send.at[k, entry], recv_sem=t_recv.at[k, slot, d],
+            device_id=at(q, region(step)), device_id_type=MESH)
+
+    def t_transit_arrival(k, entry):
+        return pltpu.make_async_remote_copy(
+            src_ref=sbuf.at[k, 0, 0], dst_ref=t_transit.at[k, entry],
+            send_sem=tt_send.at[k, entry], recv_sem=tt_recv.at[k, entry],
+            device_id=at(q + 1 - 2 * c, j), device_id_type=MESH)
+
+    def t_forward(k, act):
+        @pl.when(x == across - 1)
+        def _():
+            for slot in range(2):
+                act(t_transit_arrival(k, RIM - 1 + slot), t_onward(k, slot, RIM, RIM - 1 + slot, -RIM * across))
+
+        for d in range(1, RIM):
+            @pl.when(y >= RIM - d)
+            def _(d=d):
+                act(t_transit_arrival(k, d - 1), t_onward(k, c, d, d - 1, -RIM))
 
     def t_sibling(k):
         return pltpu.make_async_remote_copy(
@@ -190,7 +246,7 @@
     def send_windows(k, carry):
         for d in (4, 3, 2, 1, 0):
             for b in range(2):
-                col = idx_s[d, 0, 4 + 2 * b + k]
+                col = idx_s[d, 2 + b, k]
                 block = lax.shift_right_logical(col, 7)
                 offset = col & (HALF - 1)
                 first, second = strip[block], strip[block + 1]
@@ -198,7 +254,7 @@
                 sbuf[k, d, b, :, :, :HALF] = jnp.where(lane >= offset, first, third).astype(BF16)
                 sbuf[k, d, b, :, :, HALF:] = second.astype(BF16)
                 if d > 0:
-                    t_copy(k, d, b).start()
+                    t_start(k, d, b)
         t_sibling(k).start()
         t_local(k).start()
         return carry
@@ -217,8 +273,7 @@
     row = lax.broadcasted_iota(jnp.int32, (STRIP, 1), 0)
 
     def offsets(k):
-        e = 2 * c + k
-        return idx_s[0, 0, e] & (STRIP - 1), idx_s[0, 0, 4 + e] & (HALF - 1)
+        return idx_s[0, c, k] & (STRIP - 1), idx_s[0, 2 + c, k] & (HALF - 1)
 
     def window(k, slot, block, row_offset):
         if block > 0:
@@ -285,13 +340,74 @@
         z_copy(k).start()
         return carry
 
-    lax.fori_loop(0, PER, first_half, 0)
-
-    def g_copy(k, slot, d):
-        return pltpu.make_async_remote_copy(
-            src_ref=gbuf.at[k, slot, d % RIM], dst_ref=pieces.at[k, c, d],
-            send_sem=g_send.at[k, slot, d], recv_sem=g_recv.at[k, c, d],
-            device_id=at(2 * z + slot, region(d)), device_id_type=MESH)
+    def forward_windows(k):
+        def act(arrival, onward):
+            arrival.wait_recv()
+            onward.start()
+        t_forward(k, act)
+
+    def windows_and_first_half(k, carry):
+        forward_windows(k)
+        return first_half(k, carry)
+
+    lax.fori_loop(0, PER, windows_and_first_half, 0)
+
+    def g_copy(k, slot, d, target, buffer=None):
+        return pltpu.make_async_remote_copy(
+            src_ref=gbuf.at[k, slot, d % RIM], dst_ref=pieces.at[k, c, d] if buffer is None else buffer,
+            send_sem=g_send.at[k, slot, d],
+            recv_sem=g_recv.at[k, c, d] if buffer is None else gt_recv.at[k, d - 1 + c * (d // RIM)],
+            device_id=at(2 * z + slot, target), device_id_type=MESH)
+
+    def g_start(k, slot, d):
+        if d == RIM:
+            @pl.when(x == across - 1)
+            def _():
+                g_copy(k, slot, d, region(-span), g_transit.at[k, d - 1 + c]).start()
+
+            @pl.when(x < across - 1)
+            def _():
+                g_copy(k, slot, d, region(d)).start()
+            return
+
+        turned = (y + d >= RIM) & (c == slot)
+
+        @pl.when(turned)
+        def _():
+            g_copy(k, slot, d, region(d - RIM), g_transit.at[k, d - 1]).start()
+
+        @pl.when(jnp.logical_not(turned))
+        def _():
+            g_copy(k, slot, d, region(d)).start()
+
+    def g_onward(k, core, d, entry, step):
+        return pltpu.make_async_remote_copy(
+            src_ref=g_transit.at[k, entry], dst_ref=pieces.at[k, core, d],
+            send_sem=gt_send.at[k, entry], recv_sem=g_recv.at[k, core, d],
+            device_id=at(q, region(step)), device_id_type=MESH)
+
+    def g_transit_arrival(k, entry):
+        return pltpu.make_async_remote_copy(
+            src_ref=gbuf.at[k, 0, 0], dst_ref=g_transit.at[k, entry],
+            send_sem=gt_send.at[k, entry], recv_sem=gt_recv.at[k, entry],
+            device_id=at(q + 1 - 2 * c, j), device_id_type=MESH)
+
+    def g_forward(k, act):
+        @pl.when(x == 0)
+        def _():
+            for core in range(2):
+                act(g_transit_arrival(k, RIM - 1 + core), g_onward(k, core, RIM, RIM - 1 + core, RIM * across))
+
+        for d in range(1, RIM):
+            @pl.when(y < d)
+            def _(d=d):
+                act(g_transit_arrival(k, d - 1), g_onward(k, c, d, d - 1, RIM))
+
+    def forward_pieces(k):
+        def act(arrival, onward):
+            arrival.wait_recv()
+            onward.start()
+        g_forward(k, act)
 
     def g_sibling(k):
         return pltpu.make_async_remote_copy(
@@ -332,7 +448,7 @@
             gbuf[k, 1, i, 0] = gr.astype(BF16)
             gbuf[k, 1, i, 1] = (-gi).astype(BF16)
         for d in (4, 3, 2, 1):
-            g_copy(k, 1, d).start()
+            g_start(k, 1, d)
 
         @pl.when(z == 0)
         def _():
@@ -347,7 +463,7 @@
                 gbuf[k, 0, i, 1] = (-gi).astype(BF16)
 
         for d in (4, 3, 2, 1):
-            g_copy(k, 0, d).start()
+            g_start(k, 0, d)
         g_sibling(k).start()
         g_local(k).start()
 
@@ -383,6 +499,12 @@
         p_copy(2).start()
         p_copy(3).start()
         p_copy(1 - c).start()
+
+    forward_pieces(0)
+    forward_pieces(1)
+
+    @pl.when(z == 0)
+    def _():
         own = pltpu.make_async_copy(part_s.at[c], part_r.at[c], p_send.at[c])
         own.start()
         own.wait()
@@ -454,10 +576,16 @@
         g_sibling(k).wait_send()
         g_local(k).wait()
         g_arrival(k, 1 - c, 0).wait_recv()
+
+        def act(arrival, onward):
+            onward.wait_send()
+
+        t_forward(k, act)
+        g_forward(k, act)
         for d in range(1, RIM + 1):
             for b in range(2):
-                t_copy(k, d, b).wait_send()
-                g_copy(k, b, d).wait_send()
+                t_copy(k, d, b, region(-d)).wait_send()
+                g_copy(k, b, d, region(d)).wait_send()
                 g_arrival(k, b, d).wait_recv()
         return carry
 
@@ -466,23 +594,24 @@
 
 def main_call(transmission, probe, exit_adjoint, idx):
     n_scan = lax.axis_size("scan")
-    group = 16 if n_scan % 16 == 0 else 4
+    across = 4 if n_scan == 64 else 2
+    group = RIM * across
     hi_count = n_scan // group
     piece = (16 // group, 8, SIDE)
-    any_spec = pl.BlockSpec(memory_space=pl.ANY)
+    hbm_spec = pl.BlockSpec(memory_space=pltpu.HBM)
     vmem_spec = pl.BlockSpec(memory_space=pltpu.VMEM)
     field = (2, SIDE, SIDE)
     dma = pltpu.SemaphoreType.DMA
     columns = transmission.shape[3]
     return pl.pallas_call(
-        functools.partial(main_kernel, group, hi_count, n_scan),
+        functools.partial(main_kernel, across, hi_count, n_scan),
         out_shape=(
             jax.ShapeDtypeStruct((PER, 2, RIM + 1, 2, STRIP, SIDE), BF16),
             jax.ShapeDtypeStruct((RIM + 1, 8, 128), jnp.int32),
             jax.ShapeDtypeStruct((group,) + piece, F32),
         ),
-        in_specs=[any_spec] * 5,
-        out_specs=(any_spec, any_spec, vmem_spec),
+        in_specs=[hbm_spec] * 5,
+        out_specs=(hbm_spec, hbm_spec, vmem_spec),
         scratch_shapes=[
             pltpu.VMEM((columns // HALF, 2, STRIP, HALF), F32),
             pltpu.VMEM((2, 2, 2, SIDE, SIDE), BF16),
@@ -499,6 +628,8 @@
             pltpu.VMEM(field, F32),
             pltpu.VMEM((PER,) + field, BF16),
             pltpu.VMEM((PER,) + field, BF16),
+            pltpu.VMEM((PER, RIM + 1, 2, STRIP, SIDE), BF16),
+            pltpu.VMEM((PER, RIM + 1, 2, STRIP, SIDE), BF16),
             pltpu.VMEM((PER, 2, RIM, 2, STRIP, SIDE), BF16),
             pltpu.VMEM(field, F32),
             pltpu.VMEM((4, 2, STRIP, SIDE), BF16),
@@ -513,10 +644,14 @@
             dma((RIM + 1,)),
             dma((PER, RIM + 1, 2)),
             dma((PER, 2, RIM + 1)),
+            dma((PER, RIM + 1)),
+            dma((PER, RIM + 1)),
             dma((PER,)),
             dma((PER,)),
             dma((PER, 2, RIM + 1)),
             dma((PER, 2, RIM + 1)),
+            dma((PER, RIM + 1)),
+            dma((PER, RIM + 1)),
             dma((4,)),
             dma((2,)),
             dma((group,)),
@@ -544,9 +679,8 @@
         d = n // 4
         core = (n // 2) % 2
         k = n % 2
-        e = 2 * core + k
-        row_offset = idx[d, 0, e] & (STRIP - 1)
-        col = idx[d, 0, 4 + e]
+        row_offset = idx[d, core, k] & (STRIP - 1)
+        col = idx[d, 2 + core, k]
         block = lax.shift_right_logical(col, 7)
         col_offset = col & (HALF - 1)
         low = jnp.where(d == 0, row_offset, 0)
@@ -584,8 +718,7 @@
 
 
 def local(transmission, probe, exit_adjoint, scan_row, scan_col):
-    head = jnp.concatenate([scan_row.reshape(1, 4), scan_col.reshape(1, 4)], axis=1)
-    idx = jnp.pad(head, ((0, 7), (0, 120)))
+    idx = jnp.pad(jnp.concatenate([scan_row, scan_col], axis=0), ((0, 4), (0, 126)))
     pieces, idx_all, probe_sum = main_call(transmission, probe, exit_adjoint, idx)
     object_grad, probe_grad = deposit_call(idx_all, pieces, probe_sum, transmission.shape[3])
     return object_grad, probe_grad.reshape(2, STRIP, SIDE)

time: 145 us -> 92.8 us (0.64)
  Pallas kernels: 139 us -> 87.5 us
  local copies, waits for them, and re-layouts: 5.2 us -> 3.67 us
    pallas_call x1, Pallas kernels: 136 us -> 84.2 us  [main_call(): pl.pallas_call(functools.partial(main_kernel, across, hi_count, n_scan),...]
    reshape x2 -> x0, local copies, waits for them, and re-layouts: 1.52 us -> none  [the longest x1 0.76 us: local(): scan_row.reshape(1, 4)]
where the time goes in v2:
time: 92.8 us; the launch traced here: 92.6 us
  Pallas kernels  87.5 us (94%)
  local copies, waits for them, and re-layouts  3.67 us (4%)
    pallas_call x1, Pallas kernels, main_call(): pl.pallas_call(functools.partial(main_kernel, across, hi_count, n_scan),...  84.2 us
    unnamed x6, local copies, waits for them, and re-layouts  3.67 us
    pallas_call x1, Pallas kernels, deposit_call(): pl.pallas_call(deposit_kernel, out_shape=(jax.ShapeDtypeStruct((1, 2, STR...  3.33 us

profile of v2, /device:TPU:32, one launch (start us, length us, event | category | flops | bytes accessed | tf_op | source)
XLA Modules:
  0.0 92.6 jit_solution(6152605532234800457)
XLA Ops:
  0.6 0.7 pad_add_fusion
  1.3 0.0 copy-start
  1.4 1.4 %copy-done = f32[1,2,64,3072]{3,2,1,0:T(8,128)S(1)} copy-done((f32[1,2,64,3072]{3,2,1,0:T(8,128)S(1)}, f32[1,2,64,3072]{3,2,1,0:T(8,128)}, u32[]{:S(2)}) %copy-start) | copy-done | bytes 1572888
  2.8 0.0 copy-start.1
  2.8 1.0 %copy-done.1 = f32[2,256,256]{2,1,0:T(8,128)S(1)} copy-done((f32[2,256,256]{2,1,0:T(8,128)S(1)}, f32[2,256,256]{2,1,0:T(8,128)}, u32[]{:S(2)}) %copy-start.1) | copy-done | bytes 524312
  3.8 0.0 copy-start.2
  3.8 1.2 %copy-done.2 = bf16[2,2,2,256,256]{4,3,2,1,0:T(8,128)(2,1)S(1)} copy-done((bf16[2,2,2,256,256]{4,3,2,1,0:T(8,128)(2,1)S(1)}, bf16[2,2,2,256,256]{4,3,2,1,0:T(8,128)(2,1)}, u32[]{:S(2)}) %copy-start.2) | copy-done | bytes 1048600
  5.0 84.2 %waves.1 = (bf16[2,2,5,2,64,256]{5,4,3,2,1,0:T(8,128)(2,1)S(1)}, s32[5,8,128]{2,1,0:T(8,128)S(1)}, f32[16,1,8,256]{3,2,1,0:T(8,128)S(1)}) custom-call(f32[1,2,64,3072]{3,2,1,0:T(8,128)S(1)} %copy-done, f32[2,256,256]{2,1,0:T(8,128)S(1)} %copy-done.1, f32[2,2,2,256,256]{4,3,2,1,0:T(8,128)} %exit_adjoint.1, bf16[2,2,2,256,256]{4,3,2,1,0:T(8,128)(2,1)S(1)} %copy-done.2, ...), custom_call_target="tpu_custom_call" | custom-call | flops 3221225472 | bytes 8388608 | tf_op jit(solution)/shard_map/waves/pallas_call | solution.py:606
  89.2 3.3 %deposit.1 = (f32[1,2,64,3072]{3,2,1,0:T(8,128)}, f32[16,1,8,256]{3,2,1,0:T(8,128)}) custom-call(s32[5,8,128]{2,1,0:T(8,128)S(1)} %get-tuple-element.7.idx, bf16[2,2,5,2,64,256]{5,4,3,2,1,0:T(8,128)(2,1)S(1)} %get-tuple-element.8.pieces, f32[16,1,8,256]{3,2,1,0:T(8,128)S(1)} %get-tuple-element.9.probe_in), custom_call_target="tpu_custom_call" | custom-call | tf_op jit(solution)/shard_map/deposit/pallas_call | solution.py:707
  (1 shorter events, 0.0 us)
Async XLA Ops:
  1.3 1.4 %copy-start = (f32[1,2,64,3072]{3,2,1,0:T(8,128)S(1)}, f32[1,2,64,3072]{3,2,1,0:T(8,128)}, u32[]{:S(2)}) copy-start(f32[1,2,64,3072]{3,2,1,0:T(8,128)} %trans.1) | copy-start | bytes 4718596
  2.8 1.0 %copy-start.1 = (f32[2,256,256]{2,1,0:T(8,128)S(1)}, f32[2,256,256]{2,1,0:T(8,128)}, u32[]{:S(2)}) copy-start(f32[2,256,256]{2,1,0:T(8,128)} %probe.1) | copy-start | bytes 1572868
  3.8 1.2 %copy-start.2 = (bf16[2,2,2,256,256]{4,3,2,1,0:T(8,128)(2,1)S(1)}, bf16[2,2,2,256,256]{4,3,2,1,0:T(8,128)(2,1)}, u32[]{:S(2)}) copy-start(bf16[2,2,2,256,256]{4,3,2,1,0:T(8,128)(2,1)} %constant.4.clone.table_in) | copy-start | bytes 3145732

commit v3 on v2

--- a/solution.py
+++ b/solution.py
@@ -86,7 +86,7 @@
     pieces, idx_all, probe_out,
     strip, tab, probe_v, exit_v, idx_s,
     sbuf, tbuf, x_v, start_v, w1_v, w2_v, w3_v, w4_v, zsend, zrecv,
-    t_transit, g_transit, gbuf, total_v, part_s, part_r, rs_s, rs_r, ar_s, ar_r,
+    t_transit, g_transit, gbuf, total_v, part_r, rs_s, rs_r, ar_s, ar_r,
     local_sems, strip_sems, idx_send, idx_recv, t_send, t_recv, tt_send, tt_recv, z_send, z_recv,
     g_send, g_recv, gt_send, gt_recv, p_send, p_recv, rs_send, rs_recv, ar_send, ar_recv, ag_send, ag_recv,
 ):
@@ -138,7 +138,7 @@
     lax.fori_loop(0, strip.shape[0], start_strip, 0)
 
     barrier = pltpu.get_barrier_semaphore()
-    partners = [at(q + 1 - 2 * c, j), at(q + 2 - 4 * z, j), at(3 - q, j)]
+    partners = [at(q + 1 - 2 * c, j), at(q + 2 - 4 * z, j)]
     for d in range(1, RIM + 1):
         for b in range(2):
             partners.append(at(2 * z + b, region(d)))
@@ -147,6 +147,7 @@
         partners.append(at(q, mate(i)))
     for i in range(1, hi_count):
         partners.append(at(q, tier(i)))
+        partners.append(at(q + 2 - 4 * z, tier(i)))
     for device in partners:
         pl.semaphore_signal(barrier, inc=1, device_id=device, device_id_type=MESH)
     crossing = ((x == 0, span), (x == across - 1, -span))
@@ -297,7 +298,7 @@
     for copy in loads[:3]:
         copy.wait()
 
-    def first_half(k, carry):
+    def first_half(k):
         row_offset, col_offset = offsets(k)
 
         @pl.when(z == 0)
@@ -338,7 +339,6 @@
                 zsend[k, 1, rows, :] = vi.astype(BF16)
 
         z_copy(k).start()
-        return carry
 
     def forward_windows(k):
         def act(arrival, onward):
@@ -346,11 +346,6 @@
             onward.start()
         t_forward(k, act)
 
-    def windows_and_first_half(k, carry):
-        forward_windows(k)
-        return first_half(k, carry)
-
-    lax.fori_loop(0, PER, windows_and_first_half, 0)
 
     def g_copy(k, slot, d, target, buffer=None):
         return pltpu.make_async_remote_copy(
@@ -424,7 +419,7 @@
             send_sem=g_send.at[k, 0, d], recv_sem=g_recv.at[k, core, d],
             device_id=at(q + 1 - 2 * c, j), device_id_type=MESH)
 
-    def second_half(k, carry):
+    def second_half(k):
         row_offset, col_offset = offsets(k)
         z_copy(k).wait_recv()
 
@@ -478,82 +473,83 @@
                 moved = roll(x_v[ri], back_rows, back_cols)
                 total_v[ri] = jnp.where(k > 0, total_v[ri], 0.0) + moved
 
+    def position(k, carry):
+        first_half(k)
+
+        @pl.when(k == 0)
+        def _():
+            forward_windows(1)
+
+        @pl.when(k == 1)
+        def _():
+            forward_pieces(0)
+
+        second_half(k)
         return carry
 
-    lax.fori_loop(0, PER, second_half, 0)
-
-    def p_copy(section):
-        return pltpu.make_async_remote_copy(
-            src_ref=part_s.at[section], dst_ref=part_r.at[c], send_sem=p_send.at[section],
-            recv_sem=p_recv.at[c], device_id=at(section, j), device_id_type=MESH)
-
-    def p_arrival(core):
-        return pltpu.make_async_remote_copy(
-            src_ref=part_s.at[0], dst_ref=part_r.at[core], send_sem=p_send.at[0],
-            recv_sem=p_recv.at[core], device_id=at(q + 1 - 2 * c, j), device_id_type=MESH)
+    forward_windows(0)
+    lax.fori_loop(0, PER, position, 0)
+
+    def p_copy(half):
+        rows = pl.ds(pl.multiple_of((2 * half + 1 - c) * STRIP, STRIP), STRIP)
+        return pltpu.make_async_remote_copy(
+            src_ref=total_v.at[:, rows, :], dst_ref=part_r.at[half], send_sem=p_send.at[half],
+            recv_sem=p_recv.at[half], device_id=at(q + 1 - 2 * c, j), device_id_type=MESH)
+
+    def rs_copy(i):
+        return pltpu.make_async_remote_copy(
+            src_ref=rs_s.at[lax.rem(member + i, group)], dst_ref=rs_r.at[member], send_sem=rs_send.at[i],
+            recv_sem=rs_recv.at[i], device_id=at(q, mate(i)), device_id_type=MESH)
+
+    def ar_copy(half, i):
+        return pltpu.make_async_remote_copy(
+            src_ref=ar_s.at[half], dst_ref=ar_r.at[level], send_sem=ar_send.at[half, i],
+            recv_sem=ar_recv.at[i], device_id=at(c + 2 * half, tier(i)), device_id_type=MESH)
+
+    def ag_copy(i):
+        return pltpu.make_async_remote_copy(
+            src_ref=probe_out.at[member], dst_ref=probe_out.at[member], send_sem=ag_send.at[i],
+            recv_sem=ag_recv.at[i], device_id=at(q, mate(i)), device_id_type=MESH)
 
     @pl.when(z == 0)
     def _():
-        for section in range(4):
-            part_s[section] = total_v[:, section * STRIP:(section + 1) * STRIP, :].astype(BF16)
-        p_copy(2).start()
-        p_copy(3).start()
-        p_copy(1 - c).start()
-
-    forward_pieces(0)
+        for half in range(2):
+            p_copy(half).start()
+        for half in range(2):
+            p_copy(half).wait()
+            rows = pl.ds(pl.multiple_of((2 * half + c) * STRIP, STRIP), STRIP)
+            block_sum = total_v[:, rows, :] + part_r[half]
+            rs_s[:, half] = block_sum.reshape(rs_s.shape[:1] + rs_s.shape[2:])
+        for i in range(1, group):
+            rs_copy(i).start()
+        rs_r[member] = rs_s[member]
+
     forward_pieces(1)
 
     @pl.when(z == 0)
     def _():
-        own = pltpu.make_async_copy(part_s.at[c], part_r.at[c], p_send.at[c])
-        own.start()
-        own.wait()
-        p_arrival(1 - c).wait_recv()
+        for i in range(1, group):
+            rs_copy(i).wait_recv()
+        plane_sum = rs_r[0]
+        for m in range(1, group):
+            plane_sum = plane_sum + rs_r[m]
+        ar_s[...] = plane_sum
+        ar_r[level] = plane_sum[0]
+        for i in range(hi_count):
+            ar_copy(1, i).start()
+        for i in range(1, hi_count):
+            ar_copy(0, i).start()
 
     @pl.when(z == 1)
     def _():
-        p_arrival(0).wait_recv()
-        p_arrival(1).wait_recv()
-
-    block_sum = part_r[0].astype(F32) + part_r[1].astype(F32)
-    rs_s[...] = block_sum.reshape(rs_s.shape)
-
-    def rs_copy(i):
-        target = lax.rem(member + i, group)
-        return pltpu.make_async_remote_copy(
-            src_ref=rs_s.at[target], dst_ref=rs_r.at[member], send_sem=rs_send.at[i],
-            recv_sem=rs_recv.at[i], device_id=at(q, mate(i)), device_id_type=MESH)
-
-    for i in range(1, group):
-        rs_copy(i).start()
-    rs_r[member] = rs_s[member]
-    for i in range(1, group):
-        rs_copy(i).wait_recv()
-    piece_sum = rs_r[0]
-    for m in range(1, group):
-        piece_sum = piece_sum + rs_r[m]
-    ar_s[...] = piece_sum
-    ar_r[level] = piece_sum
-
-    def ar_copy(i):
-        return pltpu.make_async_remote_copy(
-            src_ref=ar_s, dst_ref=ar_r.at[level], send_sem=ar_send.at[i],
-            recv_sem=ar_recv.at[i], device_id=at(q, tier(i)), device_id_type=MESH)
+        ar_copy(1, 0).wait_recv()
 
     for i in range(1, hi_count):
-        ar_copy(i).start()
-    for i in range(1, hi_count):
-        ar_copy(i).wait()
+        ar_copy(0, i).wait_recv()
     piece_sum = ar_r[0]
     for m in range(1, hi_count):
         piece_sum = piece_sum + ar_r[m]
     probe_out[member] = piece_sum
-
-    def ag_copy(i):
-        return pltpu.make_async_remote_copy(
-            src_ref=probe_out.at[member], dst_ref=probe_out.at[member], send_sem=ag_send.at[i],
-            recv_sem=ag_recv.at[i], device_id=at(q, mate(i)), device_id_type=MESH)
-
     for i in range(1, group):
         ag_copy(i).start()
     for i in range(1, group):
@@ -561,14 +557,15 @@
 
     for copy in idx_copies:
         copy.wait_send()
-    for i in range(1, group):
-        rs_copy(i).wait_send()
 
     @pl.when(z == 0)
     def _():
-        p_copy(2).wait_send()
-        p_copy(3).wait_send()
-        p_copy(1 - c).wait_send()
+        for i in range(1, group):
+            rs_copy(i).wait_send()
+        for i in range(hi_count):
+            ar_copy(1, i).wait_send()
+        for i in range(1, hi_count):
+            ar_copy(0, i).wait_send()
 
     def drain(k, carry):
         z_copy(k).wait_send()
@@ -632,11 +629,10 @@
             pltpu.VMEM((PER, RIM + 1, 2, STRIP, SIDE), BF16),
             pltpu.VMEM((PER, 2, RIM, 2, STRIP, SIDE), BF16),
             pltpu.VMEM(field, F32),
-            pltpu.VMEM((4, 2, STRIP, SIDE), BF16),
-            pltpu.VMEM((2, 2, STRIP, SIDE), BF16),
-            pltpu.VMEM((group,) + piece, F32),
-            pltpu.VMEM((group,) + piece, F32),
-            pltpu.VMEM(piece, F32),
+            pltpu.VMEM((2, 2, STRIP, SIDE), F32),
+            pltpu.VMEM((group, 2) + piece, F32),
+            pltpu.VMEM((group, 2) + piece, F32),
+            pltpu.VMEM((2,) + piece, F32),
             pltpu.VMEM((hi_count,) + piece, F32),
             dma((6,)),
             dma((columns // HALF,)),
@@ -652,17 +648,17 @@
             dma((PER, 2, RIM + 1)),
             dma((PER, RIM + 1)),
             dma((PER, RIM + 1)),
-            dma((4,)),
+            dma((2,)),
             dma((2,)),
             dma((group,)),
             dma((group,)),
-            dma((hi_count,)),
+            dma((2, hi_count)),
             dma((hi_count,)),
             dma((group,)),
             dma((group,)),
         ],
         compiler_params=pltpu.CompilerParams(
-            collective_id=0, has_side_effects=True, vmem_limit_bytes=48 * 1024 * 1024
+            collective_id=0, has_side_effects=True, vmem_limit_bytes=62 * 1024 * 1024
         ),
         cost_estimate=pl.CostEstimate(flops=8 * 12 * 2 * SIDE**3, bytes_accessed=8 << 20, transcendentals=0),
         name="waves",
@@ -712,7 +708,7 @@
         ),
         in_specs=[pl.BlockSpec(memory_space=pltpu.SMEM), vmem_spec, vmem_spec],
         out_specs=(vmem_spec, vmem_spec),
-        compiler_params=pltpu.CompilerParams(vmem_limit_bytes=32 * 1024 * 1024),
+        compiler_params=pltpu.CompilerParams(vmem_limit_bytes=62 * 1024 * 1024),
         name="deposit",
     )(idx_all, pieces, probe_sum)
 

time: 92.8 us -> 87.3 us (0.941)
  the two profiles are of different devices: /device:TPU:32 before, /device:TPU:4 now
where the time goes in v3:
time: 87.3 us; the launch traced here: 87.1 us
  Pallas kernels  85.1 us (97%)
    pallas_call x1, Pallas kernels, main_call(): pl.pallas_call(functools.partial(main_kernel, across, hi_count, n_scan),...  81.3 us
    pallas_call x1, Pallas kernels, deposit_call(): pl.pallas_call(deposit_kernel, out_shape=(jax.ShapeDtypeStruct((1, 2, STR...  3.78 us

profile of v3, /device:TPU:4, one launch (start us, length us, event | category | flops | bytes accessed | tf_op | source)
XLA Modules:
  0.0 87.1 jit_solution(16452819147043091154)
XLA Ops:
  0.6 0.7 pad_add_fusion
  1.3 0.6 pad.4.idx_in
  1.9 81.3 %waves.1 = (bf16[2,2,5,2,64,256]{5,4,3,2,1,0:T(8,128)(2,1)}, s32[5,8,128]{2,1,0:T(8,128)}, f32[16,1,8,256]{3,2,1,0:T(8,128)}) custom-call(f32[1,2,64,3072]{3,2,1,0:T(8,128)} %trans.1, f32[2,256,256]{2,1,0:T(8,128)} %probe.1, f32[2,2,2,256,256]{4,3,2,1,0:T(8,128)} %exit_adjoint.1, bf16[2,2,2,256,256]{4,3,2,1,0:T(8,128)(2,1)} %constant.4.clone.table_in, ...), custom_call_target="tpu_custom_call" | custom-call | flops 3221225472 | bytes 8388608 | tf_op jit(solution)/shard_map/waves/pallas_call | solution.py:603
  83.3 3.8 %deposit.1 = (f32[1,2,64,3072]{3,2,1,0:T(8,128)}, f32[16,1,8,256]{3,2,1,0:T(8,128)}) custom-call(s32[5,8,128]{2,1,0:T(8,128)} %get-tuple-element.7.idx, bf16[2,2,5,2,64,256]{5,4,3,2,1,0:T(8,128)(2,1)} %get-tuple-element.8.pieces, f32[16,1,8,256]{3,2,1,0:T(8,128)} %get-tuple-element.9.probe_in), custom_call_target="tpu_custom_call" | custom-call | tf_op jit(solution)/shard_map/deposit/pallas_call | solution.py:703

commit v4 on v3

--- a/solution.py
+++ b/solution.py
@@ -85,9 +85,9 @@
     trans, probe, exit_adjoint, table_in, idx_in,
     pieces, idx_all, probe_out,
     strip, tab, probe_v, exit_v, idx_s,
-    sbuf, tbuf, x_v, start_v, w1_v, w2_v, w3_v, w4_v, zsend, zrecv,
+    xsend, xrecv, sbuf, tbuf, x_v, start_v, w1_v, w2_v, w3_v, w4_v, zsend, zrecv,
     t_transit, g_transit, gbuf, total_v, part_r, rs_s, rs_r, ar_s, ar_r,
-    local_sems, strip_sems, idx_send, idx_recv, t_send, t_recv, tt_send, tt_recv, z_send, z_recv,
+    local_sems, strip_sems, x_send, x_recv, idx_send, idx_recv, t_send, t_recv, tt_send, tt_recv, z_send, z_recv,
     g_send, g_recv, gt_send, gt_recv, p_send, p_recv, rs_send, rs_recv, ar_send, ar_recv, ag_send, ag_recv,
 ):
     q = lax.axis_index("depth")
@@ -106,6 +106,24 @@
 
     def region(step):
         return lax.rem(j + step + n_scan, n_scan)
+
+    def strip_of(core, e):
+        return e + core * (RIM - 2 * e)
+
+    def both(sign, plus, minus):
+        return ((sign > 0) & plus) | ((sign < 0) & minus)
+
+    def turns(sign, e):
+        return both(sign, y + e >= RIM, y < e)
+
+    def turned_here(sign, e):
+        return both(sign, y < e, y >= RIM - e)
+
+    def leaves(sign):
+        return both(sign, x == across - 1, x == 0)
+
+    def left_here(sign):
+        return both(sign, x == 0, x == across - 1)
 
     def mate(i):
         return level * group + lax.rem(member + i, group)
@@ -159,6 +177,11 @@
     on_edge = ((x == 0) | (x == across - 1)).astype(jnp.int32)
     pl.semaphore_wait(barrier, len(partners) + on_edge)
 
+    def x_copy(k):
+        return pltpu.make_async_remote_copy(
+            src_ref=xsend.at[k], dst_ref=xrecv.at[k], send_sem=x_send.at[k], recv_sem=x_recv.at[k],
+            device_id=at(q, region(RIM)), device_id_type=MESH)
+
     idx_copies = [
         pltpu.make_async_remote_copy(
             src_ref=idx_in, dst_ref=idx_all.at[d], send_sem=idx_send.at[d], recv_sem=idx_recv.at[d],
@@ -167,6 +190,15 @@
     ]
     for copy in idx_copies:
         copy.start()
+
+    loads[2].wait()
+
+    @pl.when((z == 1) & (c == 1))
+    def _():
+        for k in range(PER):
+            xsend[k] = exit_v[k].astype(BF16)
+            x_copy(k).start()
+
     loads[3].wait()
     for copy in idx_copies:
         copy.wait_recv()
@@ -178,35 +210,31 @@
     lane = lax.broadcasted_iota(jnp.int32, (1, 1, HALF), 2)
     last_block = strip.shape[0] - 1
 
-    def t_copy(k, d, b, target, buffer=None):
-        return pltpu.make_async_remote_copy(
-            src_ref=sbuf.at[k, d, b], dst_ref=tbuf.at[k, c, d] if buffer is None else buffer,
+    def t_copy(k, d, b, target, entry=None):
+        return pltpu.make_async_remote_copy(
+            src_ref=sbuf.at[k, d, b],
+            dst_ref=tbuf.at[k, c, d] if entry is None else t_transit.at[k, entry],
             send_sem=t_send.at[k, d, b],
-            recv_sem=t_recv.at[k, c, d] if buffer is None else tt_recv.at[k, d - 1 + c * (d // RIM)],
+            recv_sem=t_recv.at[k, c, d] if entry is None else tt_recv.at[k, entry],
             device_id=at(2 * z + b, target), device_id_type=MESH)
 
-    def t_start(k, d, b):
-        if d == RIM:
-            @pl.when(x == 0)
-            def _():
-                t_copy(k, d, b, region(span), t_transit.at[k, d - 1 + c]).start()
-
-            @pl.when(x > 0)
-            def _():
-                t_copy(k, d, b, region(-d)).start()
-            return
-
-        turned = (y < d) & (c == b)
-
-        @pl.when(turned)
-        def _():
-            t_copy(k, d, b, region(RIM - d), t_transit.at[k, d - 1]).start()
-
-        @pl.when(jnp.logical_not(turned))
-        def _():
-            t_copy(k, d, b, region(-d)).start()
-
-    def t_onward(k, slot, d, entry, step):
+    def t_start(k, e, b):
+        d, sign = strip_of(b, e), 2 * b - 1
+        if e == RIM:
+            detour, step, entry = leaves(sign), -sign * span, e - 1 + c
+        else:
+            detour, step, entry = turns(sign, e) & (c == b), -sign * (RIM - e), e - 1
+
+        @pl.when(detour)
+        def _():
+            t_copy(k, d, b, region(step), entry).start()
+
+        @pl.when(jnp.logical_not(detour))
+        def _():
+            t_copy(k, d, b, region(sign * e)).start()
+
+    def t_onward(k, slot, e, entry, step):
+        d = strip_of(c, e)
         return pltpu.make_async_remote_copy(
             src_ref=t_transit.at[k, entry], dst_ref=tbuf.at[k, slot, d],
             send_sem=tt_send.at[k, entry], recv_sem=t_recv.at[k, slot, d],
@@ -219,34 +247,40 @@
             device_id=at(q + 1 - 2 * c, j), device_id_type=MESH)
 
     def t_forward(k, act):
-        @pl.when(x == across - 1)
+        sign = 2 * c - 1
+
+        @pl.when(left_here(sign))
         def _():
             for slot in range(2):
-                act(t_transit_arrival(k, RIM - 1 + slot), t_onward(k, slot, RIM, RIM - 1 + slot, -RIM * across))
-
-        for d in range(1, RIM):
-            @pl.when(y >= RIM - d)
-            def _(d=d):
-                act(t_transit_arrival(k, d - 1), t_onward(k, c, d, d - 1, -RIM))
+                entry = RIM - 1 + slot
+                act(t_transit_arrival(k, entry), t_onward(k, slot, RIM, entry, sign * RIM * across))
+
+        for e in range(1, RIM):
+            @pl.when(turned_here(sign, e))
+            def _(e=e):
+                act(t_transit_arrival(k, e - 1), t_onward(k, c, e, e - 1, sign * RIM))
 
     def t_sibling(k):
-        return pltpu.make_async_remote_copy(
-            src_ref=sbuf.at[k, 0, 1 - c], dst_ref=tbuf.at[k, c, 0],
-            send_sem=t_send.at[k, 0, 1], recv_sem=t_recv.at[k, c, 0],
+        d = RIM * (1 - c)
+        return pltpu.make_async_remote_copy(
+            src_ref=sbuf.at[k, d, 1 - c], dst_ref=tbuf.at[k, c, d],
+            send_sem=t_send.at[k, d, 1 - c], recv_sem=t_recv.at[k, c, d],
             device_id=at(q + 1 - 2 * c, j), device_id_type=MESH)
 
     def t_local(k):
-        return pltpu.make_async_copy(sbuf.at[k, 0, c], tbuf.at[k, c, 0], t_send.at[k, 0, 0])
+        d = RIM * c
+        return pltpu.make_async_copy(sbuf.at[k, d, c], tbuf.at[k, c, d], t_send.at[k, d, c])
 
     def t_arrival(k, slot, d):
         return pltpu.make_async_remote_copy(
-            src_ref=sbuf.at[k, d, 0], dst_ref=tbuf.at[k, slot, d],
+            src_ref=sbuf.at[k, 0, 0], dst_ref=tbuf.at[k, slot, d],
             send_sem=t_send.at[k, d, 0], recv_sem=t_recv.at[k, slot, d],
             device_id=at(q + 1 - 2 * c, j), device_id_type=MESH)
 
-    def send_windows(k, carry):
-        for d in (4, 3, 2, 1, 0):
+    def send_windows(k):
+        for e in (4, 3, 2, 1, 0):
             for b in range(2):
+                d = strip_of(b, e)
                 col = idx_s[d, 2 + b, k]
                 block = lax.shift_right_logical(col, 7)
                 offset = col & (HALF - 1)
@@ -254,27 +288,24 @@
                 third = strip[jnp.minimum(block + 2, last_block)]
                 sbuf[k, d, b, :, :, :HALF] = jnp.where(lane >= offset, first, third).astype(BF16)
                 sbuf[k, d, b, :, :, HALF:] = second.astype(BF16)
-                if d > 0:
-                    t_start(k, d, b)
+                if e > 0:
+                    t_start(k, e, b)
         t_sibling(k).start()
         t_local(k).start()
-        return carry
-
-    lax.fori_loop(0, PER, send_windows, 0)
+
+    send_windows(0)
 
     def wait_windows(k):
-        for d in (0, 1, 2, 3, 4):
-            if d == 0:
-                t_local(k).wait()
-                t_arrival(k, 1 - c, 0).wait_recv()
-            else:
-                for slot in range(2):
-                    t_arrival(k, slot, d).wait_recv()
+        t_local(k).wait()
+        t_arrival(k, 1 - c, RIM * c).wait_recv()
+        for e in range(1, RIM + 1):
+            for slot in range(2):
+                t_arrival(k, slot, strip_of(c, e)).wait_recv()
 
     row = lax.broadcasted_iota(jnp.int32, (STRIP, 1), 0)
 
     def offsets(k):
-        return idx_s[0, c, k] & (STRIP - 1), idx_s[0, 2 + c, k] & (HALF - 1)
+        return idx_s[RIM * c, c, k] & (STRIP - 1), idx_s[RIM * c, 2 + c, k] & (HALF - 1)
 
     def window(k, slot, block, row_offset):
         if block > 0:
@@ -295,8 +326,13 @@
             src_ref=zsend.at[k], dst_ref=zrecv.at[k], send_sem=z_send.at[k], recv_sem=z_recv.at[k],
             device_id=at(q + 2 - 4 * z, j), device_id_type=MESH)
 
-    for copy in loads[:3]:
+    for copy in loads[:2]:
         copy.wait()
+
+    def send_later(k):
+        @pl.when(k == 0)
+        def _():
+            send_windows(1)
 
     def first_half(k):
         row_offset, col_offset = offsets(k)
@@ -306,20 +342,31 @@
             for ri in range(2):
                 start_v[k, ri] = roll(probe_v[ri], row_offset, col_offset)
             wait_windows(k)
+            send_later(k)
             for i, rows in enumerate(blocks):
                 tr, ti = window(k, 0, i, row_offset)
                 x_v[0, rows, :], x_v[1, rows, :] = times(tr, ti, start_v[k, 0, rows, :], start_v[k, 1, rows, :])
 
         @pl.when(z == 1)
         def _():
-            x_v[0] = roll(exit_v[k, 0], row_offset, col_offset)
-            x_v[1] = -roll(exit_v[k, 1], row_offset, col_offset)
+            @pl.when(c == 0)
+            def _():
+                x_v[...] = exit_v[k]
+
+            @pl.when(c == 1)
+            def _():
+                x_copy(k).wait_recv()
+                x_v[...] = xrecv[k].astype(F32)
+
+            x_v[0] = roll(x_v[0], row_offset, col_offset)
+            x_v[1] = -roll(x_v[1], row_offset, col_offset)
 
         propagate(x_v, w1_v.at[k], tab)
 
         @pl.when(z == 1)
         def _():
             wait_windows(k)
+            send_later(k)
 
         for i, rows in enumerate(blocks):
             tr, ti = window(k, 1, i, row_offset)
@@ -347,33 +394,29 @@
         t_forward(k, act)
 
 
-    def g_copy(k, slot, d, target, buffer=None):
-        return pltpu.make_async_remote_copy(
-            src_ref=gbuf.at[k, slot, d % RIM], dst_ref=pieces.at[k, c, d] if buffer is None else buffer,
-            send_sem=g_send.at[k, slot, d],
-            recv_sem=g_recv.at[k, c, d] if buffer is None else gt_recv.at[k, d - 1 + c * (d // RIM)],
+    def g_copy(k, slot, e, target, entry=None):
+        d = strip_of(c, e)
+        return pltpu.make_async_remote_copy(
+            src_ref=gbuf.at[k, slot, lax.rem(d, RIM)],
+            dst_ref=pieces.at[k, c, d] if entry is None else g_transit.at[k, entry],
+            send_sem=g_send.at[k, slot, e],
+            recv_sem=g_recv.at[k, c, d] if entry is None else gt_recv.at[k, entry],
             device_id=at(2 * z + slot, target), device_id_type=MESH)
 
-    def g_start(k, slot, d):
-        if d == RIM:
-            @pl.when(x == across - 1)
-            def _():
-                g_copy(k, slot, d, region(-span), g_transit.at[k, d - 1 + c]).start()
-
-            @pl.when(x < across - 1)
-            def _():
-                g_copy(k, slot, d, region(d)).start()
-            return
-
-        turned = (y + d >= RIM) & (c == slot)
-
-        @pl.when(turned)
-        def _():
-            g_copy(k, slot, d, region(d - RIM), g_transit.at[k, d - 1]).start()
-
-        @pl.when(jnp.logical_not(turned))
-        def _():
-            g_copy(k, slot, d, region(d)).start()
+    def g_start(k, slot, e):
+        sign = 1 - 2 * c
+        if e == RIM:
+            detour, step, entry = leaves(sign), -sign * span, e - 1 + c
+        else:
+            detour, step, entry = turns(sign, e) & (c == slot), -sign * (RIM - e), e - 1
+
+        @pl.when(detour)
+        def _():
+            g_copy(k, slot, e, region(step), entry).start()
+
+        @pl.when(jnp.logical_not(detour))
+        def _():
+            g_copy(k, slot, e, region(sign * e)).start()
 
     def g_onward(k, core, d, entry, step):
         return pltpu.make_async_remote_copy(
@@ -388,15 +431,17 @@
             device_id=at(q + 1 - 2 * c, j), device_id_type=MESH)
 
     def g_forward(k, act):
-        @pl.when(x == 0)
-        def _():
-            for core in range(2):
-                act(g_transit_arrival(k, RIM - 1 + core), g_onward(k, core, RIM, RIM - 1 + core, RIM * across))
-
-        for d in range(1, RIM):
-            @pl.when(y < d)
-            def _(d=d):
-                act(g_transit_arrival(k, d - 1), g_onward(k, c, d, d - 1, RIM))
+        for core in range(2):
+            @pl.when(left_here(1 - 2 * core))
+            def _(core=core):
+                entry, step = RIM - 1 + core, (1 - 2 * core) * RIM * across
+                act(g_transit_arrival(k, entry), g_onward(k, core, strip_of(core, RIM), entry, step))
+
+        sign = 1 - 2 * c
+        for e in range(1, RIM):
+            @pl.when(turned_here(sign, e))
+            def _(e=e):
+                act(g_transit_arrival(k, e - 1), g_onward(k, c, strip_of(c, e), e - 1, sign * RIM))
 
     def forward_pieces(k):
         def act(arrival, onward):
@@ -406,16 +451,16 @@
 
     def g_sibling(k):
         return pltpu.make_async_remote_copy(
-            src_ref=gbuf.at[k, 1 - c, 0], dst_ref=pieces.at[k, c, 0],
-            send_sem=g_send.at[k, 1, 0], recv_sem=g_recv.at[k, c, 0],
+            src_ref=gbuf.at[k, 1 - c, 0], dst_ref=pieces.at[k, c, RIM * c],
+            send_sem=g_send.at[k, 1, 0], recv_sem=g_recv.at[k, c, RIM * c],
             device_id=at(q + 1 - 2 * c, j), device_id_type=MESH)
 
     def g_local(k):
-        return pltpu.make_async_copy(gbuf.at[k, c, 0], pieces.at[k, c, 0], g_send.at[k, 0, 0])
+        return pltpu.make_async_copy(gbuf.at[k, c, 0], pieces.at[k, c, RIM * c], g_send.at[k, 0, 0])
 
     def g_arrival(k, core, d):
         return pltpu.make_async_remote_copy(
-            src_ref=gbuf.at[k, 0, d % RIM], dst_ref=pieces.at[k, core, d],
+            src_ref=gbuf.at[k, 0, 0], dst_ref=pieces.at[k, core, d],
             send_sem=g_send.at[k, 0, d], recv_sem=g_recv.at[k, core, d],
             device_id=at(q + 1 - 2 * c, j), device_id_type=MESH)
 
@@ -572,18 +617,24 @@
         t_sibling(k).wait_send()
         g_sibling(k).wait_send()
         g_local(k).wait()
-        g_arrival(k, 1 - c, 0).wait_recv()
+        g_arrival(k, 1 - c, RIM * (1 - c)).wait_recv()
 
         def act(arrival, onward):
             onward.wait_send()
 
         t_forward(k, act)
         g_forward(k, act)
-        for d in range(1, RIM + 1):
+        for e in range(1, RIM + 1):
             for b in range(2):
-                t_copy(k, d, b, region(-d)).wait_send()
-                g_copy(k, b, d, region(d)).wait_send()
+                d = strip_of(b, e)
+                t_copy(k, d, b, region(e)).wait_send()
+                g_copy(k, b, e, region(e)).wait_send()
                 g_arrival(k, b, d).wait_recv()
+
+        @pl.when((z == 1) & (c == 1))
+        def _():
+            x_copy(k).wait_send()
+
         return carry
 
     lax.fori_loop(0, PER, drain, 0)
@@ -615,6 +666,8 @@
             pltpu.VMEM(field, F32),
             pltpu.VMEM((PER,) + field, F32),
             pltpu.SMEM((RIM + 1, 8, 128), jnp.int32),
+            pltpu.VMEM((PER,) + field, BF16),
+            pltpu.VMEM((PER,) + field, BF16),
             pltpu.VMEM((PER, RIM + 1, 2, 2, STRIP, SIDE), BF16),
             pltpu.VMEM((PER, 2, RIM + 1, 2, STRIP, SIDE), BF16),
             pltpu.VMEM(field, F32),
@@ -636,6 +689,8 @@
             pltpu.VMEM((hi_count,) + piece, F32),
             dma((6,)),
             dma((columns // HALF,)),
+            dma((PER,)),
+            dma((PER,)),
             dma((RIM + 1,)),
             dma((RIM + 1,)),
             dma((PER, RIM + 1, 2)),

time: 87.3 us -> 80.1 us (0.918)
  Pallas kernels: 85.1 us -> 77.9 us
    pallas_call x1, Pallas kernels: 81.3 us -> 74.2 us  [main_call(): pl.pallas_call(functools.partial(main_kernel, across, hi_count, n_scan),...]
where the time goes in v4:
time: 80.1 us; the launch traced here: 79.9 us
  Pallas kernels  77.9 us (97%)
    pallas_call x1, Pallas kernels, main_call(): pl.pallas_call(functools.partial(main_kernel, across, hi_count, n_scan),...  74.2 us
    pallas_call x1, Pallas kernels, deposit_call(): pl.pallas_call(deposit_kernel, out_shape=(jax.ShapeDtypeStruct((1, 2, STR...  3.78 us

profile of v4, /device:TPU:4, one launch (start us, length us, event | category | flops | bytes accessed | tf_op | source)
XLA Modules:
  0.0 79.9 jit_solution(2379462403404335456)
XLA Ops:
  0.6 0.7 pad_add_fusion
  1.3 0.6 pad.4.idx_in
  1.9 74.2 %waves.1 = (bf16[2,2,5,2,64,256]{5,4,3,2,1,0:T(8,128)(2,1)}, s32[5,8,128]{2,1,0:T(8,128)}, f32[16,1,8,256]{3,2,1,0:T(8,128)}) custom-call(f32[1,2,64,3072]{3,2,1,0:T(8,128)} %trans.1, f32[2,256,256]{2,1,0:T(8,128)} %probe.1, f32[2,2,2,256,256]{4,3,2,1,0:T(8,128)} %exit_adjoint.1, bf16[2,2,2,256,256]{4,3,2,1,0:T(8,128)(2,1)} %constant.4.clone.table_in, ...), custom_call_target="tpu_custom_call" | custom-call | flops 3221225472 | bytes 8388608 | tf_op jit(solution)/shard_map/waves/pallas_call | solution.py:654
  76.1 3.8 %deposit.1 = (f32[1,2,64,3072]{3,2,1,0:T(8,128)}, f32[16,1,8,256]{3,2,1,0:T(8,128)}) custom-call(s32[5,8,128]{2,1,0:T(8,128)} %get-tuple-element.7.idx, bf16[2,2,5,2,64,256]{5,4,3,2,1,0:T(8,128)(2,1)} %get-tuple-element.8.pieces, f32[16,1,8,256]{3,2,1,0:T(8,128)} %get-tuple-element.9.probe_in), custom_call_target="tpu_custom_call" | custom-call | tf_op jit(solution)/shard_map/deposit/pallas_call | solution.py:758

commit v5 on v4

--- a/solution.py
+++ b/solution.py
@@ -82,9 +82,9 @@
 
 def main_kernel(
     across, hi_count, n_scan,
-    trans, probe, exit_adjoint, table_in, idx_in,
+    trans, probe, exit_adjoint, table_in, row_in, col_in,
     pieces, idx_all, probe_out,
-    strip, tab, probe_v, exit_v, idx_s,
+    strip, tab, probe_v, exit_v, idx_in, idx_v, idx_s,
     xsend, xrecv, sbuf, tbuf, x_v, start_v, w1_v, w2_v, w3_v, w4_v, zsend, zrecv,
     t_transit, g_transit, gbuf, total_v, part_r, rs_s, rs_r, ar_s, ar_r,
     local_sems, strip_sems, x_send, x_recv, idx_send, idx_recv, t_send, t_recv, tt_send, tt_recv, z_send, z_recv,
@@ -135,7 +135,6 @@
         pltpu.make_async_copy(table_in, tab, local_sems.at[1]),
         pltpu.make_async_copy(probe, probe_v, local_sems.at[2]),
         pltpu.make_async_copy(exit_adjoint.at[c], exit_v, local_sems.at[3]),
-        pltpu.make_async_copy(idx_in, idx_all.at[0], local_sems.at[4]),
     ]
 
     def strip_copy(i):
@@ -154,6 +153,16 @@
         return carry
 
     lax.fori_loop(0, strip.shape[0], start_strip, 0)
+
+    at_row = lax.broadcasted_iota(jnp.int32, (8, 128), 0)
+    at_lane = lax.broadcasted_iota(jnp.int32, (8, 128), 1)
+    own = jnp.zeros((8, 128), jnp.int32)
+    for b in range(BATCHES):
+        for k in range(PER):
+            own = jnp.where((at_row == b) & (at_lane == k), row_in[b, k], own)
+            own = jnp.where((at_row == 2 + b) & (at_lane == k), col_in[b, k], own)
+    idx_in[...] = own
+    idx_v[0] = own
 
     barrier = pltpu.get_barrier_semaphore()
     partners = [at(q + 1 - 2 * c, j), at(q + 2 - 4 * z, j)]
@@ -184,7 +193,7 @@
 
     idx_copies = [
         pltpu.make_async_remote_copy(
-            src_ref=idx_in, dst_ref=idx_all.at[d], send_sem=idx_send.at[d], recv_sem=idx_recv.at[d],
+            src_ref=idx_in, dst_ref=idx_v.at[d], send_sem=idx_send.at[d], recv_sem=idx_recv.at[d],
             device_id=at(q, region(d)), device_id_type=MESH)
         for d in range(1, RIM + 1)
     ]
@@ -197,13 +206,14 @@
     def _():
         for k in range(PER):
             xsend[k] = exit_v[k].astype(BF16)
-            x_copy(k).start()
-
-    loads[3].wait()
+        x_copy(0).start()
+
     for copy in idx_copies:
         copy.wait_recv()
-    to_smem = pltpu.make_async_copy(idx_all, idx_s, local_sems.at[5])
+    to_smem = pltpu.make_async_copy(idx_v, idx_s, local_sems.at[5])
     to_smem.start()
+    to_all = pltpu.make_async_copy(idx_v, idx_all, local_sems.at[4])
+    to_all.start()
     to_smem.wait()
     lax.fori_loop(0, strip.shape[0], wait_strip, 0)
 
@@ -249,16 +259,16 @@
     def t_forward(k, act):
         sign = 2 * c - 1
 
-        @pl.when(left_here(sign))
-        def _():
-            for slot in range(2):
-                entry = RIM - 1 + slot
-                act(t_transit_arrival(k, entry), t_onward(k, slot, RIM, entry, sign * RIM * across))
-
         for e in range(1, RIM):
             @pl.when(turned_here(sign, e))
             def _(e=e):
                 act(t_transit_arrival(k, e - 1), t_onward(k, c, e, e - 1, sign * RIM))
+
+        @pl.when(left_here(sign))
+        def _():
+            for slot in range(2):
+                entry = RIM - 1 + slot
+                act(t_transit_arrival(k, entry), t_onward(k, slot, RIM, entry, sign * RIM * across))
 
     def t_sibling(k):
         d = RIM * (1 - c)
@@ -295,6 +305,11 @@
 
     send_windows(0)
 
+    @pl.when((z == 1) & (c == 1))
+    def _():
+        x_copy(1).start()
+
+
     def wait_windows(k):
         t_local(k).wait()
         t_arrival(k, 1 - c, RIM * c).wait_recv()
@@ -600,6 +615,7 @@
     for i in range(1, group):
         ag_copy(i).wait()
 
+    to_all.wait()
     for copy in idx_copies:
         copy.wait_send()
 
@@ -640,7 +656,7 @@
     lax.fori_loop(0, PER, drain, 0)
 
 
-def main_call(transmission, probe, exit_adjoint, idx):
+def main_call(transmission, probe, exit_adjoint, scan_row, scan_col):
     n_scan = lax.axis_size("scan")
     across = 4 if n_scan == 64 else 2
     group = RIM * across
@@ -658,13 +674,15 @@
             jax.ShapeDtypeStruct((RIM + 1, 8, 128), jnp.int32),
             jax.ShapeDtypeStruct((group,) + piece, F32),
         ),
-        in_specs=[hbm_spec] * 5,
+        in_specs=[hbm_spec] * 4 + [pl.BlockSpec(memory_space=pltpu.SMEM)] * 2,
         out_specs=(hbm_spec, hbm_spec, vmem_spec),
         scratch_shapes=[
             pltpu.VMEM((columns // HALF, 2, STRIP, HALF), F32),
             pltpu.VMEM((2, 2, 2, SIDE, SIDE), BF16),
             pltpu.VMEM(field, F32),
             pltpu.VMEM((PER,) + field, F32),
+            pltpu.VMEM((8, 128), jnp.int32),
+            pltpu.VMEM((RIM + 1, 8, 128), jnp.int32),
             pltpu.SMEM((RIM + 1, 8, 128), jnp.int32),
             pltpu.VMEM((PER,) + field, BF16),
             pltpu.VMEM((PER,) + field, BF16),
@@ -717,7 +735,7 @@
         ),
         cost_estimate=pl.CostEstimate(flops=8 * 12 * 2 * SIDE**3, bytes_accessed=8 << 20, transcendentals=0),
         name="waves",
-    )(transmission, probe, exit_adjoint, jnp.asarray(tables()), idx)
+    )(transmission, probe, exit_adjoint, jnp.asarray(tables()), scan_row, scan_col)
 
 
 def deposit_kernel(idx, pieces, probe_in, grad, probe_out):
@@ -769,8 +787,7 @@
 
 
 def local(transmission, probe, exit_adjoint, scan_row, scan_col):
-    idx = jnp.pad(jnp.concatenate([scan_row, scan_col], axis=0), ((0, 4), (0, 126)))
-    pieces, idx_all, probe_sum = main_call(transmission, probe, exit_adjoint, idx)
+    pieces, idx_all, probe_sum = main_call(transmission, probe, exit_adjoint, scan_row, scan_col)
     object_grad, probe_grad = deposit_call(idx_all, pieces, probe_sum, transmission.shape[3])
     return object_grad, probe_grad.reshape(2, STRIP, SIDE)
 

time: 80.1 us -> 78.8 us (0.984)
  no operation moved by 1% of the time
where the time goes in v5:
time: 78.8 us; the launch traced here: 78.6 us
  Pallas kernels  78 us (99%)
    pallas_call x1, Pallas kernels, main_call(): pl.pallas_call(functools.partial(main_kernel, across, hi_count, n_scan),...  74.2 us
    pallas_call x1, Pallas kernels, deposit_call(): pl.pallas_call(deposit_kernel, out_shape=(jax.ShapeDtypeStruct((1, 2, STR...  3.78 us

profile of v5, /device:TPU:4, one launch (start us, length us, event | category | flops | bytes accessed | tf_op | source)
XLA Modules:
  0.0 78.6 jit_solution(7628402497663330504)
XLA Ops:
  0.6 74.2 %waves.1 = (bf16[2,2,5,2,64,256]{5,4,3,2,1,0:T(8,128)(2,1)}, s32[5,8,128]{2,1,0:T(8,128)}, f32[16,1,8,256]{3,2,1,0:T(8,128)}) custom-call(f32[1,2,64,3072]{3,2,1,0:T(8,128)} %trans.1, f32[2,256,256]{2,1,0:T(8,128)} %probe.1, f32[2,2,2,256,256]{4,3,2,1,0:T(8,128)} %exit_adjoint.1, bf16[2,2,2,256,256]{4,3,2,1,0:T(8,128)(2,1)} %constant.2.clone.table_in, ...), custom_call_target="tpu_custom_call" | custom-call | flops 3221225472 | bytes 8388608 | tf_op jit(solution)/shard_map/waves/pallas_call | solution.py:670
  74.9 3.8 %deposit.1 = (f32[1,2,64,3072]{3,2,1,0:T(8,128)}, f32[16,1,8,256]{3,2,1,0:T(8,128)}) custom-call(s32[5,8,128]{2,1,0:T(8,128)} %get-tuple-element.7.idx, bf16[2,2,5,2,64,256]{5,4,3,2,1,0:T(8,128)(2,1)} %get-tuple-element.8.pieces, f32[16,1,8,256]{3,2,1,0:T(8,128)} %get-tuple-element.9.probe_in), custom_call_target="tpu_custom_call" | custom-call | tf_op jit(solution)/shard_map/deposit/pallas_call | solution.py:776

commit v6 on v5

--- a/solution.py
+++ b/solution.py
@@ -575,11 +575,13 @@
     def _():
         for half in range(2):
             p_copy(half).start()
+        halves = []
         for half in range(2):
             p_copy(half).wait()
             rows = pl.ds(pl.multiple_of((2 * half + c) * STRIP, STRIP), STRIP)
             block_sum = total_v[:, rows, :] + part_r[half]
-            rs_s[:, half] = block_sum.reshape(rs_s.shape[:1] + rs_s.shape[2:])
+            halves.append(block_sum.reshape(group, rs_s.shape[1] // 2, SIDE))
+        rs_s[...] = jnp.concatenate(halves, axis=1).astype(BF16)
         for i in range(1, group):
             rs_copy(i).start()
         rs_r[member] = rs_s[member]
@@ -590,9 +592,10 @@
     def _():
         for i in range(1, group):
             rs_copy(i).wait_recv()
-        plane_sum = rs_r[0]
+        plane_sum = rs_r[0].astype(F32)
         for m in range(1, group):
-            plane_sum = plane_sum + rs_r[m]
+            plane_sum = plane_sum + rs_r[m].astype(F32)
+        plane_sum = plane_sum.reshape(ar_s.shape)
         ar_s[...] = plane_sum
         ar_r[level] = plane_sum[0]
         for i in range(hi_count):
@@ -701,8 +704,8 @@
             pltpu.VMEM((PER, 2, RIM, 2, STRIP, SIDE), BF16),
             pltpu.VMEM(field, F32),
             pltpu.VMEM((2, 2, STRIP, SIDE), F32),
-            pltpu.VMEM((group, 2) + piece, F32),
-            pltpu.VMEM((group, 2) + piece, F32),
+            pltpu.VMEM((group, 16 * piece[0], SIDE), BF16),
+            pltpu.VMEM((group, 16 * piece[0], SIDE), BF16),
             pltpu.VMEM((2,) + piece, F32),
             pltpu.VMEM((hi_count,) + piece, F32),
             dma((6,)),

time: 78.8 us -> 78.2 us (level)
  Pallas kernels: 78 us -> 76.7 us
    pallas_call x1, Pallas kernels: 74.2 us -> 73 us  [main_call(): pl.pallas_call(functools.partial(main_kernel, across, hi_count, n_scan),...]
where the time goes in v6:
time: 78.2 us; the launch traced here: 77.4 us
  Pallas kernels  76.7 us (98%)
    pallas_call x1, Pallas kernels, main_call(): pl.pallas_call(functools.partial(main_kernel, across, hi_count, n_scan),...  73 us
    pallas_call x1, Pallas kernels, deposit_call(): pl.pallas_call(deposit_kernel, out_shape=(jax.ShapeDtypeStruct((1, 2, STR...  3.78 us

profile of v6, /device:TPU:4, one launch (start us, length us, event | category | flops | bytes accessed | tf_op | source)
XLA Modules:
  0.0 77.4 jit_solution(11727651424766003890)
XLA Ops:
  0.6 73.0 %waves.1 = (bf16[2,2,5,2,64,256]{5,4,3,2,1,0:T(8,128)(2,1)}, s32[5,8,128]{2,1,0:T(8,128)}, f32[16,1,8,256]{3,2,1,0:T(8,128)}) custom-call(f32[1,2,64,3072]{3,2,1,0:T(8,128)} %trans.1, f32[2,256,256]{2,1,0:T(8,128)} %probe.1, f32[2,2,2,256,256]{4,3,2,1,0:T(8,128)} %exit_adjoint.1, bf16[2,2,2,256,256]{4,3,2,1,0:T(8,128)(2,1)} %constant.2.clone.table_in, ...), custom_call_target="tpu_custom_call" | custom-call | flops 3221225472 | bytes 8388608 | tf_op jit(solution)/shard_map/waves/pallas_call | solution.py:673
  73.6 3.8 %deposit.1 = (f32[1,2,64,3072]{3,2,1,0:T(8,128)}, f32[16,1,8,256]{3,2,1,0:T(8,128)}) custom-call(s32[5,8,128]{2,1,0:T(8,128)} %get-tuple-element.7.idx, bf16[2,2,5,2,64,256]{5,4,3,2,1,0:T(8,128)(2,1)} %get-tuple-element.8.pieces, f32[16,1,8,256]{3,2,1,0:T(8,128)} %get-tuple-element.9.probe_in), custom_call_target="tpu_custom_call" | custom-call | tf_op jit(solution)/shard_map/deposit/pallas_call | solution.py:779
